TPU v7x, 32 devices: a whole 2x2x4 slice. The times are simulated.
32 devices in a mesh: tm: 8 (over y, x, core), row: 4 (over z).
Axes of the slice: x: 2, y: 2, z: 4, core: 2. Of those that a mesh axis runs over, the one named last changes fastest.
Arguments:
- frames_in: bfloat16 [16, 16, 64, 256], P('tm', 'row'), may hold values from -6 to 6
- cotangent: bfloat16 [16, 16, 64, 256], P('tm', 'row'), may hold values from -6 to 6
- kernel: bfloat16 [9, 256, 256], replicated, may hold values from -0.125 to 0.125
- readout: bfloat16 [256, 256], replicated, may hold values from -0.375 to 0.375
- feedthrough: float32 [256], replicated, may hold values from 0.5 to 1.5
- decay_rate: float32 [16, 256], P('tm'), may hold values from 0.05 to 1, as said below
- start_state: float32 [16, 64, 256], P('row'), may hold values from -6 to 6
Outputs:
- grad_frames: bfloat16 [16, 16, 64, 256], P('tm', 'row')
- grad_kernel: float32 [9, 256, 256], P(None, 'row')
- grad_readout: float32 [256, 256], P(None, 'row')
Inputs may be any that keep to these rules, and one draw needn't show every extreme that they name: `decay_rate`: every entry lies strictly between 0 and 1.
All inputs are finite; a program needn't handle non-finite values.
Results may differ from a plain program's by a relative error of at most 0.015.
Values may be sent and summed in bfloat16 or wider, within the bound.
A program may use at most 64 MiB of HBM per device.

v0:
```python
import math

import jax
import jax.numpy as jnp
from jax import lax
from jax.sharding import PartitionSpec as P

SQRT_TWO_PI = 0.7978845608
CUBIC = 0.044715


def extended(cells, sides, width):
    for axis, dim in sides:
        count = lax.axis_size(axis)
        ends = count - 1
        head = lax.slice_in_dim(cells, 0, width, axis=dim)
        tail = lax.slice_in_dim(cells, cells.shape[dim] - width, cells.shape[dim], axis=dim)
        cells = jnp.concatenate(
            [
                lax.ppermute(tail, axis, [(i, (i + 1) % count) for i in range(ends)]),
                cells,
                lax.ppermute(head, axis, [((i + 1) % count, i) for i in range(ends)]),
            ],
            axis=dim,
        )
    return cells


def carried_in(value, axis, join, neutral, backward):
    count, mine = (lax.axis_size(axis), lax.axis_index(axis))
    pieces = jax.tree.map(lambda part: lax.all_gather(part, axis), value)
    if backward:
        pieces = jax.tree.map(lambda part: part[::-1], pieces)
        mine = count - 1 - mine
    subtotal = jax.tree.map(
        lambda part, zero: jnp.full_like(part, 0) + jnp.asarray(zero, part.dtype), value, neutral
    )

    def turn(position, subtotal):
        longer = join(subtotal, jax.tree.map(lambda part: part[position], pieces))
        return jax.tree.map(lambda new, old: jnp.where(position < mine, new, old), longer, subtotal)

    return lax.fori_loop(0, count - 1, turn, subtotal)


def gelu_slope(mixture):
    inside = SQRT_TWO_PI * (mixture + CUBIC * mixture * mixture * mixture)
    tangent = jnp.tanh(inside)
    return 0.5 * (1.0 + tangent) + 0.5 * mixture * (1.0 - tangent * tangent) * SQRT_TWO_PI * (
        1.0 + 3.0 * CUBIC * mixture * mixture
    )


def block_taps(padded, band_rows, grid_width, flipped):
    pieces = []
    for vertical in range(3):
        for lateral in range(3):
            from_top = 2 - vertical if flipped else vertical
            from_left = 2 - lateral if flipped else lateral
            pieces.append(
                padded[:, from_top : from_top + band_rows, from_left : from_left + grid_width, :]
            )
    return jnp.stack(pieces, axis=3)


def compose(earlier, later):
    return (later[0] * earlier[0], later[0] * earlier[1] + later[1])


def local(frames_in, cotangent, kernel, readout, feedthrough, decay_rate, start_state):
    frames_here, band_rows, grid_width, channels = frames_in.shape
    state_width = kernel.shape[2]
    cell_count = frames_here * band_rows * grid_width
    rimmed = extended(frames_in, (("row", 1),), 1)
    padded = jnp.pad(rimmed, ((0, 0), (0, 0), (1, 1), (0, 0)))
    input_taps = block_taps(padded, band_rows, grid_width, False).reshape(cell_count, 9 * channels)
    driven = jnp.dot(
        input_taps, kernel.reshape(9 * channels, state_width), preferred_element_type=jnp.float32
    )
    driven = driven.reshape(frames_here, band_rows, grid_width, state_width)
    gain_all = jnp.sqrt(1.0 - decay_rate * decay_rate)
    leader = (lax.axis_index("tm") == 0).astype(jnp.float32)

    def advance(carried, inputs):
        driven_now, rate_now, gain_now = inputs
        carried = rate_now * carried + gain_now * driven_now
        return (carried, carried)

    _, local_states = lax.scan(advance, start_state * leader, (driven, decay_rate, gain_all))
    through = jnp.cumprod(decay_rate, axis=0)
    identity = (
        jnp.ones((state_width,), jnp.float32),
        jnp.zeros((band_rows, grid_width, state_width), jnp.float32),
    )
    _, entering = carried_in((through[-1], local_states[-1]), "tm", compose, identity, False)
    states = local_states + through[:, None, None, :] * entering[None]
    state_bf = states.astype(jnp.bfloat16).reshape(cell_count, state_width)
    mixture = jnp.dot(state_bf, readout, preferred_element_type=jnp.float32)
    slope_bf = (
        cotangent.reshape(cell_count, channels).astype(jnp.float32) * gelu_slope(mixture)
    ).astype(jnp.bfloat16)
    pulled = lax.dot_general(
        slope_bf, readout, (((1,), (1,)), ((), ())), preferred_element_type=jnp.float32
    )
    pulled = pulled.reshape(frames_here, band_rows, grid_width, state_width)
    later_rate = jnp.concatenate([decay_rate[1:], jnp.ones((1, state_width), jnp.float32)], axis=0)

    def retreat(carried, inputs):
        pulled_now, rate_next = inputs
        carried = pulled_now + rate_next * carried
        return (carried, carried)

    _, local_adjoint = lax.scan(
        retreat,
        jnp.zeros((band_rows, grid_width, state_width), jnp.float32),
        (pulled, later_rate),
        reverse=True,
    )
    remaining = jnp.flip(jnp.cumprod(jnp.flip(later_rate, 0), axis=0), 0)
    _, arriving = carried_in(
        (through[-1], decay_rate[0][None, None, :] * local_adjoint[0]),
        "tm",
        compose,
        identity,
        True,
    )
    adjoint = local_adjoint + remaining[:, None, None, :] * arriving[None]
    grad_drive = (gain_all[:, None, None, :] * adjoint).astype(jnp.bfloat16)
    rim_adjoint = extended(grad_drive, (("row", 1),), 1)
    padded_drive = jnp.pad(rim_adjoint, ((0, 0), (0, 0), (1, 1), (0, 0)))
    output_taps = block_taps(padded_drive, band_rows, grid_width, True).reshape(
        cell_count, 9, state_width
    )
    spread = lax.dot_general(
        output_taps, kernel, (((1, 2), (0, 2)), ((), ())), preferred_element_type=jnp.float32
    )
    spread = spread.reshape(frames_here, band_rows, grid_width, channels)
    grad_frames = (spread + feedthrough * cotangent.astype(jnp.float32)).astype(jnp.bfloat16)
    kernel_term = lax.dot_general(
        input_taps,
        grad_drive.reshape(cell_count, state_width),
        (((0,), (0,)), ((), ())),
        preferred_element_type=jnp.float32,
    ).reshape(9, channels, state_width)
    readout_term = lax.dot_general(
        state_bf, slope_bf, (((0,), (0,)), ((), ())), preferred_element_type=jnp.float32
    )
    band_count = lax.axis_size("row")
    scaling = 1.0 / math.sqrt(cell_count * lax.axis_size("tm") * band_count)
    kernel_band, readout_band = (
        lax.psum_scatter(
            kernel_term.astype(jnp.bfloat16), "row", scatter_dimension=1, tiled=True
        ).astype(jnp.float32),
        lax.psum_scatter(
            readout_term.astype(jnp.bfloat16), "row", scatter_dimension=1, tiled=True
        ).astype(jnp.float32),
    )
    kernel_part, readout_part = (
        lax.psum(kernel_band.astype(jnp.bfloat16), "tm").astype(jnp.float32),
        lax.psum(readout_band.astype(jnp.bfloat16), "tm").astype(jnp.float32),
    )
    return (grad_frames, kernel_part * scaling, readout_part * scaling)


def solution(mesh):
    placed = (
        P("tm", "row", None, None),
        P("tm", "row", None, None),
        P(),
        P(),
        P(),
        P("tm", None),
        P("row", None, None),
    )
    return jax.shard_map(
        local,
        mesh=mesh,
        in_specs=placed,
        out_specs=(P("tm", "row", None, None), P(None, "row", None), P(None, "row")),
        check_vma=False,
    )
```

profile of v0, /device:TPU:0, one launch (start us, length us, event | category | flops | bytes accessed | tf_op | source)
XLA Modules:
  0.0 219.2 jit_solution(13474227317324938255)
XLA Ops:
  7.2 1.0 fusion.42
  8.2 4.9 %collective-permute-start = (bf16[2,1,64,256]{3,2,1,0:T(8,128)(2,1)S(1)}, bf16[2,1,64,256]{3,2,1,0:T(8,128)(2,1)S(1)}, u32[]{:S(2)}, u32[]{:S(2)}) collective-permute-start(bf16[2,1,64,256]{3,2,1,0:T(8,128)(2,1)S(1)} %get-tuple-element.434), channel_id=1, source_target_pairs={{0,1},{1,2},{2,3},{4,5},{5,6},{6,7},{8,9},{9,10},{10,11},{12,13},{... | collective-permute-start | bytes 196616 | tf_op jit(solution)/shard_map/ppermute | solution.py:20
  13.2 1.3 collective-permute-start.1
  14.5 1.0 broadcast_multiply_fusion
  16.2 3.2 %collective-permute-done.1 = bf16[2,1,64,256]{3,2,1,0:T(8,128)(2,1)S(1)} collective-permute-done((bf16[2,1,64,256]{3,2,1,0:T(8,128)(2,1)S(1)}, bf16[2,1,64,256]{3,2,1,0:T(8,128)(2,1)S(1)}, u32[]{:S(2)}, u32[]{:S(2)}) %collective-permute-start.1) | collective-permute-done | bytes 65568 | tf_op jit(solution)/shard_map/ppermute | solution.py:22
  19.3 1.1 fusion.19
  20.4 1.0 fusion.38
  21.8 0.8 convolution_bitcast_fusion.1
  24.4 8.9 %all-gather = f32[8,1,256]{2,1,0:T(1,128)S(1)} all-gather(f32[1,1,256]{2,1,0:T(1,128)S(1)} %slice_bitcast_fusion.12), channel_id=1, replica_groups=mesh['tm'=8,'row'=4] {'tm'}, dimensions={0}, use_global_device_ids=true | all-gather | bytes 9216 | tf_op jit(solution)/shard_map/all_gather | solution.py:31
  33.3 19.3 %all-gather.4.cloned.1.call-done = f32[8,4,64,256]{3,2,1,0:T(8,128)} async-done(((f32[1,4,64,256]{3,2,1,0:T(8,128)}), f32[8,4,64,256]{3,2,1,0:T(8,128)}) %all-gather.4.cloned.1.call-update) | async-done | bytes 2097168 | tf_op jit(solution)/shard_map/all_gather | solution.py:31
  52.5 8.3 %while.58 = (s32[]{:T(128)}, f32[4,64,256]{2,1,0:T(8,128)S(1)}, s32[]{:T(128)}, f32[8,256]{1,0:T(8,128)S(1)}, f32[8,4,64,256]{3,2,1,0:T(8,128)}, /*index=5*/s32[]{:T(128)}, s32[]{:T(128)}) while((s32[]{:T(128)}, f32[4,64,256]{2,1,0:T(8,128)S(1)}, s32[]{:T(128)}, f32[8,256]{1,0:T(8,128)S(1)}, f32[8,4,64,256]{3,2,1,0:T(8,128)}, ...), condition=%wide.region_4.5_spmd.clone, body=%wide.region_3.4_spmd.clone.sunk | while | flops 262148 | bytes 789609 | solution.py:43
  52.6 1.2 fusion.57
  53.8 1.1 fusion.57
  55.0 1.1 fusion.57
  56.2 1.1 fusion.57
  57.3 1.1 fusion.57
  58.5 1.1 fusion.57
  59.7 1.1 fusion.57
  61.7 0.9 convolution_convert_fusion.1
  64.2 3.3 %copy.51 = bf16[2,4,64,9,256]{4,3,2,1,0:T(8,128)(2,1)S(1)} copy(bf16[2,4,64,9,256]{4,2,3,1,0:T(8,128)(2,1)} %copy-done.2) | data formatting | bytes 4718592 | tf_op jit(solution)/shard_map/stack | solution.py:63
  67.5 2.7 %copy.57 = bf16[64,8,9,256]{3,1,2,0:T(8,128)(2,1)} copy(bf16[64,8,9,256]{3,2,1,0:T(8,128)(2,1)S(1)} %bitcast.183) | data formatting | bytes 4718592
  70.2 4.3 %copy.52 = bf16[2304,512]{1,0:T(8,128)(2,1)} copy(bf16[2304,512]{0,1:T(8,128)(2,1)} %bitcast.184) | data formatting | bytes 4718592 | tf_op jit(solution)/shard_map/dot_general | solution.py:139
  74.5 7.6 %reduce-scatter.5.cloned.1.call-done = bf16[256,64]{0,1:T(8,128)(2,1)} async-done(((bf16[256,256]{0,1:T(8,128)(2,1)}), bf16[256,64]{0,1:T(8,128)(2,1)}) %reduce-scatter.5.cloned.1.call-update) | async-done | bytes 32784 | tf_op jit(solution)/shard_map/reduce_scatter | solution.py:154
  82.1 23.1 %psum.15 = bf16[256,64]{0,1:T(8,128)(2,1)S(1)} all-reduce(bf16[256,64]{0,1:T(8,128)(2,1)} %reduce-scatter.5.cloned.1.call-done), channel_id=1, replica_groups=mesh['tm'=8,'row'=4] {'tm'}, use_global_device_ids=true, to_apply=%region_13.14 | all-reduce | flops 16384 | bytes 65536 | tf_op jit(solution)/shard_map/psum | solution.py:160
  105.2 5.7 %all-gather.6.cloned.1.call-done = f32[8,4,64,256]{3,2,1,0:T(8,128)} async-done(((f32[1,4,64,256]{3,2,1,0:T(8,128)}), f32[8,4,64,256]{3,2,1,0:T(8,128)}) %all-gather.6.cloned.1.call-update) | async-done | bytes 2097168 | tf_op jit(solution)/shard_map/all_gather | solution.py:31
  110.9 3.1 %rev.16 = f32[8,4,64,256]{3,2,1,0:T(8,128)} reverse(f32[8,4,64,256]{3,2,1,0:T(8,128)} %all-gather.6.cloned.1.call-done), dimensions={0} | reverse | bytes 4194304 | tf_op jit(solution)/shard_map/rev | solution.py:33
  114.0 8.3 %while.60 = (s32[]{:T(128)}, f32[4,64,256]{2,1,0:T(8,128)S(1)}, s32[]{:T(128)}, f32[8,256]{1,0:T(8,128)S(1)}, f32[8,4,64,256]{3,2,1,0:T(8,128)}, /*index=5*/s32[]{:T(128)}, s32[]{:T(128)}) while((s32[]{:T(128)}, f32[4,64,256]{2,1,0:T(8,128)S(1)}, s32[]{:T(128)}, f32[8,256]{1,0:T(8,128)S(1)}, f32[8,4,64,256]{3,2,1,0:T(8,128)}, ...), condition=%wide.region_9.10_spmd.clone, body=%wide.region_8.9_spmd.clone.sunk | while | flops 262148 | bytes 789609 | solution.py:43
  114.0 1.1 fusion.58
  115.2 1.1 fusion.58
  116.4 1.1 fusion.58
  117.6 1.1 fusion.58
  118.8 1.1 fusion.58
  120.0 1.1 fusion.58
  121.2 1.1 fusion.58
  122.4 3.5 %convolution_convert_fusion = bf16[9,256,256]{2,1,0:T(8,128)(2,1)} fusion(bf16[9,256,512]{2,1,0:T(8,128)(2,1)} %bitcast.185, bf16[512,256,1]{1,0,2:T(8,128)(2,1)S(1)} %bitcast.186), kind=kOutput, calls=%fused_computation.15 | convolution fusion | flops 604569600 | bytes 3801088 | tf_op jit(solution)/shard_map/dot_general | solution.py:139
  126.0 3.3 %collective-permute-start.2 = (bf16[2,1,64,256]{3,2,1,0:T(8,128)(2,1)S(1)}, bf16[2,1,64,256]{3,2,1,0:T(8,128)(2,1)S(1)}, u32[]{:S(2)}, u32[]{:S(2)}) collective-permute-start(bf16[2,1,64,256]{3,2,1,0:T(8,128)(2,1)S(1)} %get-tuple-element.432), channel_id=1, source_target_pairs={{0,1},{1,2},{2,3},{4,5},{5,6},{6,7},{8,9},{9,10},{10,11},{12,13},{... | collective-permute-start | bytes 196616 | tf_op jit(solution)/shard_map/ppermute | solution.py:20
  129.3 1.3 collective-permute-start.3
  131.3 6.3 %collective-permute-done.3 = bf16[2,1,64,256]{3,2,1,0:T(8,128)(2,1)S(1)} collective-permute-done((bf16[2,1,64,256]{3,2,1,0:T(8,128)(2,1)S(1)}, bf16[2,1,64,256]{3,2,1,0:T(8,128)(2,1)S(1)}, u32[]{:S(2)}, u32[]{:S(2)}) %collective-permute-start.3) | collective-permute-done | bytes 65568 | tf_op jit(solution)/shard_map/ppermute | solution.py:22
  137.7 0.8 fusion.29
  139.9 0.8 fusion.25
  140.7 0.8 bitcast_dynamic-update-slice_fusion.2
  142.2 0.8 fusion.23
  143.1 0.8 fusion.22
  143.8 0.7 fusion.20
  144.6 11.7 %reduce-scatter.3.cloned.1.call-done = bf16[9,64,256]{2,1,0:T(8,128)(2,1)} async-done(((bf16[9,256,256]{2,1,0:T(8,128)(2,1)}), bf16[9,64,256]{2,1,0:T(8,128)(2,1)}) %reduce-scatter.3.cloned.1.call-update) | async-done | bytes 294928 | tf_op jit(solution)/shard_map/reduce_scatter | solution.py:151
  156.3 3.2 %fusion.4 = bf16[2,4,64,256]{3,2,1,0:T(8,128)(2,1)} fusion(bf16[2,4,64,9,256]{4,2,3,1,0:T(8,128)(2,1)} %fusion.20, bf16[9,256,256]{2,1,0:T(8,128)(2,1)S(1)} %copy-done, f32[256]{0:T(256)S(1)} %copy-done.6, bf16[2,4,64,256]{3,2,1,0:T(8,128)(2,1)S(1)} %copy-done.5), kind=kOutput, calls=%fused_computation.21 | convolution fusion | flops 604504064 | bytes 4064256 | tf_op jit(solution)/shard_map/dot_general | solution.py:134
  159.4 51.4 %all-reduce.5.cloned.1.call-done = bf16[9,64,256]{2,1,0:T(8,128)(2,1)} async-done(((bf16[9,64,256]{2,1,0:T(8,128)(2,1)}), bf16[9,64,256]{2,1,0:T(8,128)(2,1)}) %all-reduce.5.cloned.1.call-update) | async-done | bytes 294928 | tf_op jit(solution)/shard_map/psum | solution.py:159
  210.8 1.8 convert_multiply_fusion
  (85 shorter events, 8.8 us)
Async XLA Ops:
  7.2 14.6 %copy-start = (bf16[9,256,256]{2,1,0:T(8,128)(2,1)S(1)}, bf16[9,256,256]{2,1,0:T(8,128)(2,1)}, u32[]{:S(2)}) copy-start(bf16[9,256,256]{2,1,0:T(8,128)(2,1)} %param.17) | copy-start | bytes 3538948
  7.2 14.3 %copy-start.1 = (bf16[2,4,64,256]{3,2,1,0:T(8,128)(2,1)S(1)}, bf16[2,4,64,256]{3,2,1,0:T(8,128)(2,1)}, u32[]{:S(2)}) copy-start(bf16[2,4,64,256]{3,2,1,0:T(8,128)(2,1)} %param.15) | copy-start | bytes 786436
  7.2 45.3 %all-gather.4.cloned.1.call-start = ((), (), s32[]{:S(2)}) async-start(), calls=%async_computation.2 | async-start | bytes 2359296 | tf_op jit(solution)/shard_map/all_gather | solution.py:31
  8.2 7.9 %collective-permute-start = (bf16[2,1,64,256]{3,2,1,0:T(8,128)(2,1)S(1)}, bf16[2,1,64,256]{3,2,1,0:T(8,128)(2,1)S(1)}, u32[]{:S(2)}, u32[]{:S(2)}) collective-permute-start(bf16[2,1,64,256]{3,2,1,0:T(8,128)(2,1)S(1)} %get-tuple-element.434), channel_id=1, source_target_pairs={{0,1},{1,2},{2,3},{4,5},{5,6},{6,7},{8,9},{9,10},{10,11},{12,13},{... | collective-permute-start | bytes 196616 | tf_op jit(solution)/shard_map/ppermute | solution.py:20
  13.2 6.2 %collective-permute-start.1 = (bf16[2,1,64,256]{3,2,1,0:T(8,128)(2,1)S(1)}, bf16[2,1,64,256]{3,2,1,0:T(8,128)(2,1)S(1)}, u32[]{:S(2)}, u32[]{:S(2)}) collective-permute-start(bf16[2,1,64,256]{3,2,1,0:T(8,128)(2,1)S(1)} %get-tuple-element.435), channel_id=1, source_target_pairs={{1,0},{2,1},{3,2},{5,4},{6,5},{7,6},{9,8},{10,9},{11,10},{13,12},{... | collective-permute-start | bytes 196616 | tf_op jit(solution)/shard_map/ppermute | solution.py:22
  21.7 1.4 copy-start.2
  21.8 1.4 copy-start.4
  24.2 57.8 %reduce-scatter.5.cloned.1.call-start = ((), (), s32[]{:S(2)}) async-start(), calls=%async_computation.6 | async-start | bytes 163840 | tf_op jit(solution)/shard_map/reduce_scatter | solution.py:154
  52.5 8.4 %copy-start.3 = (bf16[256,256]{1,0:T(8,128)(2,1)S(1)}, bf16[256,256]{1,0:T(8,128)(2,1)}, u32[]{:S(2)}) copy-start(bf16[256,256]{1,0:T(8,128)(2,1)} %param.18) | copy-start | bytes 393220
  52.5 8.4 %copy-start.5 = (bf16[2,4,64,256]{3,2,1,0:T(8,128)(2,1)S(1)}, bf16[2,4,64,256]{3,2,1,0:T(8,128)(2,1)}, u32[]{:S(2)}) copy-start(bf16[2,4,64,256]{3,2,1,0:T(8,128)(2,1)} %param.16) | copy-start | bytes 786436
  62.7 48.2 %all-gather.6.cloned.1.call-start = ((), (), s32[]{:S(2)}) async-start(), calls=%async_computation.3 | async-start | bytes 2359296 | tf_op jit(solution)/shard_map/all_gather | solution.py:31
  63.9 92.4 %reduce-scatter.3.cloned.1.call-start = ((), (), s32[]{:S(2)}) async-start(), calls=%async_computation.4 | async-start | bytes 1474560 | tf_op jit(solution)/shard_map/reduce_scatter | solution.py:151
  125.9 84.9 %all-reduce.5.cloned.1.call-start = ((), (), s32[]{:S(2)}) async-start(), calls=%async_computation.5 | async-start | bytes 589824 | tf_op jit(solution)/shard_map/psum | solution.py:159
  126.0 5.3 %collective-permute-start.2 = (bf16[2,1,64,256]{3,2,1,0:T(8,128)(2,1)S(1)}, bf16[2,1,64,256]{3,2,1,0:T(8,128)(2,1)S(1)}, u32[]{:S(2)}, u32[]{:S(2)}) collective-permute-start(bf16[2,1,64,256]{3,2,1,0:T(8,128)(2,1)S(1)} %get-tuple-element.432), channel_id=1, source_target_pairs={{0,1},{1,2},{2,3},{4,5},{5,6},{6,7},{8,9},{9,10},{10,11},{12,13},{... | collective-permute-start | bytes 196616 | tf_op jit(solution)/shard_map/ppermute | solution.py:20
  129.3 8.2 %collective-permute-start.3 = (bf16[2,1,64,256]{3,2,1,0:T(8,128)(2,1)S(1)}, bf16[2,1,64,256]{3,2,1,0:T(8,128)(2,1)S(1)}, u32[]{:S(2)}, u32[]{:S(2)}) collective-permute-start(bf16[2,1,64,256]{3,2,1,0:T(8,128)(2,1)S(1)} %get-tuple-element.433), channel_id=1, source_target_pairs={{1,0},{2,1},{3,2},{5,4},{6,5},{7,6},{9,8},{10,9},{11,10},{13,12},{... | collective-permute-start | bytes 196616 | tf_op jit(solution)/shard_map/ppermute | solution.py:22
  139.2 17.1 %copy-start.6 = (f32[256]{0:T(256)S(1)}, f32[256]{0:T(256)}, u32[]{:S(2)}) copy-start(f32[256]{0:T(256)} %param.19) | copy-start | bytes 3076
Sparse Core Ops, SparseCore 0:
  24.4 28.1 all-gather.3
  62.8 19.1 reduce-scatter.4
  84.7 26.1 all-gather.5
  126.0 30.1 reduce-scatter.2
  159.5 51.3 all-reduce.4
where the time goes:
time: 220 us; the launch traced here: 219 us
  waiting for transfers between devices  105 us (48%)
  blocking collectives  32 us (15%)
  other arithmetic  26.1 us (12%)
  local copies, waits for them, and re-layouts  21.1 us (10%)
  between operations  14.1 us (6%)
  starting transfers between devices  11.1 us (5%)
  matrix products  9.15 us (4%)
    psum x1, waiting for transfers between devices, local(): lax.psum(kernel_band.astype(jnp.bfloat16), 'tm').astype(jnp.float32)  51.4 us
    all_gather x2, waiting for transfers between devices, carried_in(): pieces = jax.tree.map(lambda part: lax.all_gather(part, axis), value)  25 us
    psum x1, blocking collectives, local(): lax.psum(readout_band.astype(jnp.bfloat16), 'tm').astype(jnp.float32)  23.1 us
    select_n x14, other arithmetic, turn(): jnp.where(position < mine, new, old)  16.1 us
    reduce_scatter x1, waiting for transfers between devices, local(): lax.psum_scatter(kernel_term.astype(jnp.bfloat16), 'row', scatter_dimensi...  11.7 us
    ppermute x2, waiting for transfers between devices, extended(): lax.ppermute(head, axis, [((i + 1) % count, i) for i in range(ends)])  9.45 us
    all_gather x1, blocking collectives, carried_in(): pieces = jax.tree.map(lambda part: lax.all_gather(part, axis), value)  8.89 us
    ppermute x2, starting transfers between devices, extended(): lax.ppermute(tail, axis, [(i, (i + 1) % count) for i in range(ends)])  8.28 us
  transfers between devices with their start and end apart: 9, of which 7 were waited for; matrix products, arithmetic and copies ran while one was open for 11% of the time, Pallas kernels for 0%

commit v1 on v0

v1 whole, which is shorter than its diff:
```python
import functools
import math

import jax
import jax.numpy as jnp
from jax import lax
from jax.experimental import pallas as pl
from jax.experimental.pallas import tpu as pltpu
from jax.sharding import PartitionSpec as P

SQRT_TWO_PI = 0.7978845608
CUBIC = 0.044715
F32 = jnp.float32
BF16 = jnp.bfloat16
MESH = pl.DeviceIdType.MESH


def gelu_slope(mixture):
    square = mixture * mixture
    tangent = jnp.tanh(SQRT_TWO_PI * (mixture + CUBIC * square * mixture))
    return 0.5 * (1.0 + tangent) + 0.5 * mixture * (1.0 - tangent * tangent) * SQRT_TWO_PI * (
        1.0 + 3.0 * CUBIC * square
    )


def place(taps, frame, padded_row, cells, rows, width):
    channels = cells.shape[1]
    wide = cells.astype(F32)
    column = lax.broadcasted_iota(jnp.int32, wide.shape, 0)
    before = jnp.where(column == 0, 0.0, pltpu.roll(wide, 1, 0)).astype(BF16)
    after = jnp.where(column == width - 1, 0.0, pltpu.roll(wide, width - 1, 0)).astype(BF16)
    for j, shifted in enumerate((before, cells, after)):
        for i in range(3):
            h = padded_row - i
            if 0 <= h < rows:
                k = 3 * i + j
                taps[
                    pl.ds((frame * rows + h) * width, width), pl.ds(k * channels, channels)
                ] = shifted


def pieces(start, size, block):
    done = 0
    while done < size:
        at = start + done
        length = min(size - done, block - at % block)
        yield at // block, at % block, done, length
        done += length


def fused(
    dims,
    frames, cotangent, kernel, readout, feedthrough, decay, start_state,
    grad_frames, grad_kernel, grad_readout,
    taps, taps_t, kernel_t, drive_taps,
    halo, drive_halo, own_decay, all_decay,
    cot_send, cot_recv, driven, drv_send, drv_recv,
    states_bf, slopes, pulled, gd_send, gd_recv, drive,
    grads, pair_recv, chip_send, chip_recv, total, row_send, row_recv, final,
    halo_ss, halo_rs, dec_ss, dec_rs, cot_ss, cot_rs, drv_ss, drv_rs, gd_ss, gd_rs,
    dhalo_ss, dhalo_rs, pair_ss, pair_rs, chip_ss, chip_rs, row_ss, row_rs, fin_ss, fin_rs,
):
    n, nz, tap_rows = dims
    frames_here, rows, width, channels = frames.shape
    state_width = kernel.shape[1]
    band_cells = rows * width
    share = band_cells // n
    chips = n // 2
    half = state_width // 2
    me = lax.axis_index("tm")
    band = lax.axis_index("row")
    core = lax.rem(me, 2)
    chip = lax.div(me, 2)

    def remote(src, dst, send_sem, recv_sem, where):
        return pltpu.make_async_remote_copy(
            src_ref=src, dst_ref=dst, send_sem=send_sem, recv_sem=recv_sem,
            device_id=where, device_id_type=MESH,
        )

    barrier = pltpu.get_barrier_semaphore()
    for d in range(1, n):
        pl.semaphore_signal(
            barrier, inc=1, device_id={"tm": lax.rem(me + d, n)}, device_id_type=MESH
        )
    for d in range(1, nz):
        pl.semaphore_signal(
            barrier, inc=1, device_id={"row": lax.rem(band + d, nz)}, device_id_type=MESH
        )

    own_decay[...] = jnp.zeros_like(own_decay)
    own_decay[0:frames_here, :] = decay[...]
    all_decay[me] = own_decay[...]
    for s in range(n):
        cot_send[s] = jnp.concatenate(
            [cotangent[f, s * share : (s + 1) * share, :] for f in range(frames_here)], axis=0
        )
    cot_recv[me] = cot_send[me]
    pl.semaphore_wait(barrier, (n - 1) + (nz - 1))

    def edge_copies(src, dst, ss, rs):
        up = remote(src.at[:, 0], dst.at[1], ss.at[0], rs.at[1], {"row": band - 1})
        down = remote(src.at[:, rows - 1], dst.at[0], ss.at[1], rs.at[0], {"row": band + 1})
        return up, down

    def edge_start(src, dst, ss, rs):
        up, down = edge_copies(src, dst, ss, rs)

        @pl.when(band > 0)
        def _():
            up.start()

        @pl.when(band < nz - 1)
        def _():
            down.start()

        @pl.when(band == 0)
        def _():
            dst[0] = jnp.zeros(dst.shape[1:], BF16)

        @pl.when(band == nz - 1)
        def _():
            dst[1] = jnp.zeros(dst.shape[1:], BF16)

    def edge_wait(src, dst, ss, rs, arrived):
        up, down = edge_copies(src, dst, ss, rs)

        @pl.when(band > 0)
        def _():
            if arrived:
                down.wait_recv()
            else:
                up.wait_send()

        @pl.when(band < nz - 1)
        def _():
            if arrived:
                up.wait_recv()
            else:
                down.wait_send()

    edge_start(frames, halo, halo_ss, halo_rs)

    def over_tm(src_of, dst, ss, rs):
        copies = []
        for d in range(1, n):
            to = lax.rem(me + d, n)
            copies.append(
                remote(src_of(to), dst.at[me], ss.at[d - 1], rs.at[d - 1], {"tm": to})
            )
        return copies

    dec_copies = over_tm(lambda to: own_decay, all_decay, dec_ss, dec_rs)
    cot_copies = over_tm(lambda to: cot_send.at[to], cot_recv, cot_ss, cot_rs)
    for copy in dec_copies + cot_copies:
        copy.start()

    for f in range(frames_here):
        for r in range(rows):
            place(taps, f, r + 1, frames[f, r], rows, width)
    edge_wait(frames, halo, halo_ss, halo_rs, True)
    for f in range(frames_here):
        place(taps, f, 0, halo[0, f], rows, width)
        place(taps, f, rows + 1, halo[1, f], rows, width)
    driven[...] = jnp.dot(taps[...], kernel[...], preferred_element_type=F32)
    for s in range(n):
        drv_send[s] = jnp.concatenate(
            [
                driven[f * band_cells + s * share : f * band_cells + (s + 1) * share, :]
                for f in range(frames_here)
            ],
            axis=0,
        ).astype(BF16)
    drv_copies = over_tm(lambda to: drv_send.at[to], drv_recv, drv_ss, drv_rs)
    for copy in drv_copies:
        copy.start()
    drv_recv[me] = drv_send[me]

    for k in range(9):
        taps_t[pl.ds(k * channels, channels), :] = taps[:, pl.ds(k * channels, channels)].T
        kernel_t[pl.ds(k * state_width, state_width), :] = kernel[
            pl.ds((8 - k) * channels, channels), :
        ].T

    for copy in dec_copies + drv_copies:
        copy.wait_recv()
    state = start_state[pl.ds(pl.multiple_of(me * share, share), share), :]
    for s in range(n):
        arrived = drv_recv[s].astype(F32)
        kept = []
        for f in range(frames_here):
            rate = all_decay[s, f : f + 1, :]
            gain = jnp.sqrt(1.0 - rate * rate)
            state = rate * state + gain * arrived[f * share : (f + 1) * share]
            kept.append(state)
        states_bf[s] = jnp.concatenate(kept, axis=0).astype(BF16)
    for copy in cot_copies:
        copy.wait_recv()
    flat = n * frames_here * share
    flat_states = states_bf[...].reshape(flat, state_width)
    mixture = jnp.dot(flat_states, readout[...], preferred_element_type=F32)
    slopes[...] = (
        cot_recv[...].reshape(flat, channels).astype(F32) * gelu_slope(mixture)
    ).astype(BF16)
    pulled[...] = lax.dot_general(
        slopes[...], readout[...], (((1,), (1,)), ((), ())), preferred_element_type=F32
    )
    adjoint = jnp.zeros((share, state_width), F32)
    rate = jnp.zeros((1, state_width), F32)
    for s in reversed(range(n)):
        kept = []
        for f in reversed(range(frames_here)):
            at = (s * frames_here + f) * share
            adjoint = pulled[at : at + share, :] + rate * adjoint
            rate = all_decay[s, f : f + 1, :]
            kept.append(jnp.sqrt(1.0 - rate * rate) * adjoint)
        gd_send[s] = jnp.concatenate(kept[::-1], axis=0).astype(BF16)
    gd_copies = over_tm(lambda to: gd_send.at[to], gd_recv, gd_ss, gd_rs)
    for copy in gd_copies:
        copy.start()
    gd_recv[me] = gd_send[me]

    rows_here = channels // nz
    block = tap_rows * rows_here // chips

    def keep(k, product):
        rounded = product.astype(BF16)
        for z in range(nz):
            for j, offset, at, length in pieces(k * rows_here, rows_here, block):
                begin = z * rows_here + at
                for h in range(2):
                    grads[h, j, z, pl.ds(offset, length), :] = rounded[
                        begin : begin + length, h * half : (h + 1) * half
                    ]

    keep(
        9,
        lax.dot_general(
            slopes[...], flat_states, (((0,), (0,)), ((), ())), preferred_element_type=F32
        ),
    )
    for k in range(10, tap_rows):
        keep(k, jnp.zeros((channels, state_width), F32))
    for copy in gd_copies:
        copy.wait_recv()
    for f in range(frames_here):
        drive[f] = (
            jnp.concatenate(
                [gd_recv[s, f * share : (f + 1) * share, :].astype(F32) for s in range(n)], axis=0
            )
            .astype(BF16)
            .reshape(rows, width, state_width)
        )
    edge_start(drive, drive_halo, dhalo_ss, dhalo_rs)
    flat_drive = drive[...].reshape(frames_here * band_cells, state_width)
    for k in range(9):
        keep(
            k,
            jnp.dot(
                taps_t[pl.ds(k * channels, channels), :], flat_drive, preferred_element_type=F32
            ),
        )

    pair_copies = []
    for d in list(range(1, chips)) + [0]:
        j = lax.rem(chip + d, chips)
        pair_copies.append(
            remote(
                grads.at[1 - core, j], pair_recv.at[j], pair_ss.at[d], pair_rs.at[d],
                {"tm": me + 1 - 2 * core},
            )
        )
        pair_copies[-1].start()
    for f in range(frames_here):
        for r in range(rows):
            place(drive_taps, f, r + 1, drive[f, r], rows, width)

    chip_copies = []
    for d in range(1, chips):
        j = lax.rem(chip + d, chips)
        pair_copies[d - 1].wait_recv()
        chip_send[d - 1] = (grads[core, j].astype(F32) + pair_recv[j].astype(F32)).astype(BF16)
        chip_copies.append(
            remote(
                chip_send.at[d - 1], chip_recv.at[d - 1], chip_ss.at[d - 1], chip_rs.at[d - 1],
                {"tm": 2 * j + core},
            )
        )
        chip_copies[-1].start()
    pair_copies[-1].wait_recv()
    total[...] = grads[core, chip].astype(F32) + pair_recv[chip].astype(F32)

    edge_wait(drive, drive_halo, dhalo_ss, dhalo_rs, True)
    for f in range(frames_here):
        place(drive_taps, f, 0, drive_halo[0, f], rows, width)
        place(drive_taps, f, rows + 1, drive_halo[1, f], rows, width)
    spread = jnp.dot(drive_taps[...], kernel_t[...], preferred_element_type=F32)
    for f in range(frames_here):
        grad_frames[f] = (
            spread[f * band_cells : (f + 1) * band_cells]
            + feedthrough[...] * cotangent[f].astype(F32)
        ).astype(BF16)

    for copy in chip_copies:
        copy.wait_recv()
    summed = total[...]
    for d in range(1, chips):
        summed = summed + chip_recv[d - 1].astype(F32)
    total[...] = summed
    row_send[...] = summed.astype(BF16)

    row_copies = []
    for d in range(1, nz):
        z = lax.rem(band + d, nz)
        row_copies.append(
            remote(
                row_send.at[z], row_recv.at[d - 1], row_ss.at[d - 1], row_rs.at[d - 1], {"row": z}
            )
        )
        row_copies[-1].start()
    for copy in row_copies:
        copy.wait_recv()
    mine = total[band]
    for d in range(1, nz):
        mine = mine + row_recv[d - 1].astype(F32)
    final[me] = mine.astype(BF16)

    fin_copies = over_tm(lambda to: final.at[me], final, fin_ss, fin_rs)
    for copy in fin_copies:
        copy.start()
    for copies in (dec_copies, cot_copies, drv_copies, gd_copies, pair_copies, chip_copies):
        for copy in copies:
            copy.wait_send()
    edge_wait(frames, halo, halo_ss, halo_rs, False)
    edge_wait(drive, drive_halo, dhalo_ss, dhalo_rs, False)
    for copy in row_copies:
        copy.wait_send()
    for copy in fin_copies:
        copy.wait_recv()
    scaling = 1.0 / math.sqrt(frames_here * band_cells * n * nz)
    for k in range(10):
        for j, offset, at, length in pieces(k * rows_here, rows_here, block):
            for h in range(2):
                value = final[2 * j + h, pl.ds(offset, length), :].astype(F32) * scaling
                lanes = pl.ds(h * half, half)
                if k < 9:
                    grad_kernel[k, pl.ds(at, length), lanes] = value
                else:
                    grad_readout[pl.ds(at, length), lanes] = value
    for copy in fin_copies:
        copy.wait_send()


def local(n, nz, frames_in, cotangent, kernel, readout, feedthrough, decay_rate, start_state):
    frames_here, rows, width, channels = frames_in.shape
    state_width = kernel.shape[2]
    cells = rows * width
    share = cells // n
    chips = n // 2
    rows_here = channels // nz
    half = state_width // 2
    tap_rows = 10
    while tap_rows * rows_here % (16 * chips):
        tap_rows += 1
    block = tap_rows * rows_here // chips
    mixed = frames_here * share
    vmem = pltpu.VMEM
    dma = pltpu.SemaphoreType.DMA
    whole = pl.BlockSpec(memory_space=pltpu.VMEM)
    every = frames_here * cells
    scratch = [
        vmem((every, 9 * channels), BF16),
        vmem((9 * channels, every), BF16),
        vmem((9 * state_width, channels), BF16),
        vmem((every, 9 * state_width), BF16),
        vmem((2, frames_here, width, channels), BF16),
        vmem((2, frames_here, width, state_width), BF16),
        vmem((8, state_width), F32),
        vmem((n, 8, state_width), F32),
        vmem((n, mixed, channels), BF16),
        vmem((n, mixed, channels), BF16),
        vmem((every, state_width), F32),
        vmem((n, mixed, state_width), BF16),
        vmem((n, mixed, state_width), BF16),
        vmem((n, mixed, state_width), BF16),
        vmem((n * mixed, channels), BF16),
        vmem((n * mixed, state_width), F32),
        vmem((n, mixed, state_width), BF16),
        vmem((n, mixed, state_width), BF16),
        vmem((frames_here, rows, width, state_width), BF16),
        vmem((2, chips, nz, block, half), BF16),
        vmem((chips, nz, block, half), BF16),
        vmem((chips - 1, nz, block, half), BF16),
        vmem((chips - 1, nz, block, half), BF16),
        vmem((nz, block, half), F32),
        vmem((nz, block, half), BF16),
        vmem((nz - 1, block, half), BF16),
        vmem((n, block, half), BF16),
    ]
    for count in (2, n - 1, n - 1, n - 1, n - 1, 2, chips, chips - 1, nz - 1, n - 1):
        scratch += [dma((count,)), dma((count,))]
    spread, kernel_part, readout_part = pl.pallas_call(
        functools.partial(fused, (n, nz, tap_rows)),
        out_shape=(
            jax.ShapeDtypeStruct((frames_here, cells, channels), BF16),
            jax.ShapeDtypeStruct((9, rows_here, state_width), F32),
            jax.ShapeDtypeStruct((rows_here, state_width), F32),
        ),
        in_specs=[whole] * 7,
        out_specs=(whole, whole, whole),
        scratch_shapes=scratch,
        compiler_params=pltpu.CompilerParams(
            collective_id=0, has_side_effects=True, vmem_limit_bytes=48 * 1024 * 1024
        ),
        cost_estimate=pl.CostEstimate(
            flops=2 * every * channels * state_width * 30,
            bytes_accessed=6 * 1024 * 1024,
            transcendentals=every * channels,
        ),
        name="conv_s5_backward",
    )(
        frames_in,
        cotangent.reshape(frames_here, cells, channels),
        kernel.reshape(9 * channels, state_width),
        readout,
        feedthrough.reshape(1, channels),
        decay_rate,
        start_state.reshape(cells, state_width),
    )
    return (spread.reshape(frames_in.shape), kernel_part, readout_part.T)


def solution(mesh):
    placed = (
        P("tm", "row", None, None),
        P("tm", "row", None, None),
        P(),
        P(),
        P(),
        P("tm", None),
        P("row", None, None),
    )
    return jax.shard_map(
        functools.partial(local, mesh.shape["tm"], mesh.shape["row"]),
        mesh=mesh,
        in_specs=placed,
        out_specs=(P("tm", "row", None, None), P(None, "row", None), P(None, "row")),
        check_vma=False,
    )
```

time: 220 us -> 52.2 us (0.24)
  waiting for transfers between devices: 105 us -> 0 us
  Pallas kernels: 0 us -> 42.7 us
  blocking collectives: 32 us -> 0 us
  other arithmetic: 26.1 us -> 0 us
  between operations: 14.1 us -> 0.66 us
  local copies, waits for them, and re-layouts: 21.1 us -> 8.52 us
  starting transfers between devices: 11.1 us -> 0 us
  matrix products: 9.15 us -> 0 us
    psum x1 -> x0, waiting for transfers between devices: 51.4 us -> none  [local(): lax.psum(kernel_band.astype(jnp.bfloat16), 'tm').astype(jnp.float32)]
    pallas_call x0 -> x1, Pallas kernels: none -> 42.7 us  [local(): pl.pallas_call(functools.partial(fused, (n, nz, tap_rows)), out_shape=(ja...]
    all_gather x2 -> x0, waiting for transfers between devices: 25 us -> none  [carried_in(): pieces = jax.tree.map(lambda part: lax.all_gather(part, axis), value)]
    psum x1 -> x0, blocking collectives: 23.1 us -> none  [local(): lax.psum(readout_band.astype(jnp.bfloat16), 'tm').astype(jnp.float32)]
    reduce_scatter x2 -> x0, waiting for transfers between devices: 19.2 us -> none  [the longest x1 11.7 us: local(): lax.psum_scatter(kernel_term.astype(jnp.bfloat16), 'row', scatter_dimensi...]
    select_n x14 -> x0, other arithmetic: 16.1 us -> none  [turn(): jnp.where(position < mine, new, old)]
    ppermute x4 -> x0, starting transfers between devices: 10.9 us -> none  [the longest x2 8.28 us: extended(): lax.ppermute(tail, axis, [(i, (i + 1) % count) for i in range(ends)])]
    ppermute x4 -> x0, waiting for transfers between devices: 9.45 us -> none  [the longest x2 9.45 us: extended(): lax.ppermute(head, axis, [((i + 1) % count, i) for i in range(ends)])]
  transfers between devices with their start and end apart: 9 -> 0, of which waited for: 7 -> 0; matrix products, arithmetic and copies ran while one was open for 11% -> 0% of each run, Pallas kernels for 0% -> 0%
where the time goes in v1:
time: 52.2 us; the launch traced here: 51.9 us
  Pallas kernels  42.7 us (82%)
  local copies, waits for them, and re-layouts  8.52 us (16%)
  between operations  0.66 us (1%)
    pallas_call x1, Pallas kernels, local(): pl.pallas_call(functools.partial(fused, (n, nz, tap_rows)), out_shape=(ja...  42.7 us
    unnamed x17, local copies, waits for them, and re-layouts  8.52 us

profile of v1, /device:TPU:0, one launch (start us, length us, event | category | flops | bytes accessed | tf_op | source)
XLA Modules:
  0.0 51.9 jit_solution(11639214194572277672)
XLA Ops:
  0.6 0.0 copy-start
  0.6 1.3 %copy-done = bf16[9,256,256]{2,1,0:T(8,128)(2,1)S(1)} copy-done((bf16[9,256,256]{2,1,0:T(8,128)(2,1)S(1)}, bf16[9,256,256]{2,1,0:T(8,128)(2,1)}, u32[]{:S(2)}) %copy-start) | copy-done | bytes 1179672
  1.9 0.0 copy-start.1
  1.9 0.9 %copy-done.1 = bf16[2,4,64,256]{3,2,1,0:T(8,128)(2,1)S(1)} copy-done((bf16[2,4,64,256]{3,2,1,0:T(8,128)(2,1)S(1)}, bf16[2,4,64,256]{3,2,1,0:T(8,128)(2,1)}, u32[]{:S(2)}) %copy-start.1) | copy-done | bytes 262168
  2.9 0.0 copy-start.2
  2.9 0.9 %copy-done.2 = bf16[2,4,64,256]{3,2,1,0:T(8,128)(2,1)S(1)} copy-done((bf16[2,4,64,256]{3,2,1,0:T(8,128)(2,1)S(1)}, bf16[2,4,64,256]{3,2,1,0:T(8,128)(2,1)}, u32[]{:S(2)}) %copy-start.2) | copy-done | bytes 262168
  3.8 0.0 copy-start.3
  3.8 0.9 %copy-done.3 = f32[4,64,256]{2,1,0:T(8,128)S(1)} copy-done((f32[4,64,256]{2,1,0:T(8,128)S(1)}, f32[4,64,256]{2,1,0:T(8,128)}, u32[]{:S(2)}) %copy-start.3) | copy-done | bytes 262168
  4.8 0.0 copy-start.4
  4.8 0.9 %copy-done.4 = bf16[256,256]{1,0:T(8,128)(2,1)S(1)} copy-done((bf16[256,256]{1,0:T(8,128)(2,1)S(1)}, bf16[256,256]{1,0:T(8,128)(2,1)}, u32[]{:S(2)}) %copy-start.4) | copy-done | bytes 131096
  5.7 0.0 copy-start.5
  5.7 0.7 %copy-done.5 = f32[2,256]{1,0:T(2,128)S(1)} copy-done((f32[2,256]{1,0:T(2,128)S(1)}, f32[2,256]{1,0:T(2,128)}, u32[]{:S(2)}) %copy-start.5) | copy-done | bytes 2072
  6.3 0.0 copy-start.6
  6.3 0.7 %copy-done.6 = f32[256]{0:T(256)S(1)} copy-done((f32[256]{0:T(256)S(1)}, f32[256]{0:T(256)}, u32[]{:S(2)}) %copy-start.6) | copy-done | bytes 1048
  7.0 42.7 %conv_s5_backward.1 = (bf16[2,256,256]{2,1,0:T(8,128)(2,1)S(1)}, f32[9,64,256]{2,1,0:T(8,128)S(1)}, f32[64,256]{1,0:T(8,128)S(1)}) custom-call(bf16[2,4,64,256]{3,2,1,0:T(8,128)(2,1)S(1)} %copy-done.1, bf16[2,256,256]{2,1,0:T(8,128)(2,1)S(1)} %bitcast.9, bf16[2304,256]{1,0:T(8,128)(2,1)S(1)} %bitcast.8, bf16[256,256]{1,0:T(8,128)(2,1)S(1)} %copy-done.4, ...), custom_call_target="tpu_custom_call" | custom-call | flops 2013265920 | bytes 6291456 | tf_op jit(solution)/shard_map/conv_s5_backward/pallas_call | solution.py:402
  49.7 0.7 %copy.13 = bf16[2,4,64,256]{3,2,1,0:T(8,128)(2,1)} copy(bf16[2,4,64,256]{3,2,1,0:T(8,128)(2,1)S(1)} %bitcast.6) | data formatting | bytes 524288
  50.4 0.8 %copy.14 = f32[9,64,256]{2,1,0:T(8,128)} copy(f32[9,64,256]{2,1,0:T(8,128)S(1)} %get-tuple-element.13) | data formatting | bytes 1179648
  51.3 0.6 %copy.15 = f32[256,64]{0,1:T(8,128)} copy(f32[256,64]{0,1:T(8,128)S(1)} %bitcast.7) | data formatting | bytes 131072
Async XLA Ops:
  0.6 1.3 %copy-start = (bf16[9,256,256]{2,1,0:T(8,128)(2,1)S(1)}, bf16[9,256,256]{2,1,0:T(8,128)(2,1)}, u32[]{:S(2)}) copy-start(bf16[9,256,256]{2,1,0:T(8,128)(2,1)} %param.9) | copy-start | bytes 3538948
  1.9 0.9 %copy-start.1 = (bf16[2,4,64,256]{3,2,1,0:T(8,128)(2,1)S(1)}, bf16[2,4,64,256]{3,2,1,0:T(8,128)(2,1)}, u32[]{:S(2)}) copy-start(bf16[2,4,64,256]{3,2,1,0:T(8,128)(2,1)} %frames.1) | copy-start | bytes 786436
  2.9 0.9 %copy-start.2 = (bf16[2,4,64,256]{3,2,1,0:T(8,128)(2,1)S(1)}, bf16[2,4,64,256]{3,2,1,0:T(8,128)(2,1)}, u32[]{:S(2)}) copy-start(bf16[2,4,64,256]{3,2,1,0:T(8,128)(2,1)} %param.8) | copy-start | bytes 786436
  3.8 0.9 %copy-start.3 = (f32[4,64,256]{2,1,0:T(8,128)S(1)}, f32[4,64,256]{2,1,0:T(8,128)}, u32[]{:S(2)}) copy-start(f32[4,64,256]{2,1,0:T(8,128)} %param.13) | copy-start | bytes 786436
  4.8 0.9 %copy-start.4 = (bf16[256,256]{1,0:T(8,128)(2,1)S(1)}, bf16[256,256]{1,0:T(8,128)(2,1)}, u32[]{:S(2)}) copy-start(bf16[256,256]{1,0:T(8,128)(2,1)} %readout.1) | copy-start | bytes 393220
  5.7 0.7 %copy-start.5 = (f32[2,256]{1,0:T(2,128)S(1)}, f32[2,256]{1,0:T(2,128)}, u32[]{:S(2)}) copy-start(f32[2,256]{1,0:T(2,128)} %decay.1) | copy-start | bytes 6148
  6.3 0.7 %copy-start.6 = (f32[256]{0:T(256)S(1)}, f32[256]{0:T(256)}, u32[]{:S(2)}) copy-start(f32[256]{0:T(256)} %param.11) | copy-start | bytes 3076

commit v2 on v1

--- a/solution.py
+++ b/solution.py
@@ -50,17 +50,32 @@
 
 def fused(
     dims,
-    frames, cotangent, kernel, readout, feedthrough, decay, start_state,
+    frames_hbm, cotangent_hbm, kernel_hbm, readout_hbm, feedthrough_hbm, decay_hbm, start_hbm,
     grad_frames, grad_kernel, grad_readout,
+    frames, cotangent, kernel, readout, feedthrough, decay, start_state, load_sems,
     taps, taps_t, kernel_t, drive_taps,
     halo, drive_halo, own_decay, all_decay,
     cot_send, cot_recv, driven, drv_send, drv_recv,
     states_bf, slopes, pulled, gd_send, gd_recv, drive,
-    grads, pair_recv, chip_send, chip_recv, total, row_send, row_recv, final,
+    grads_a, grads_b, pair_a, pair_b, send1_a, send1_b, recv1_a, recv1_b, total_a, total_b,
+    send2_a, send2_b, recv2_a, recv2_b, final,
     halo_ss, halo_rs, dec_ss, dec_rs, cot_ss, cot_rs, drv_ss, drv_rs, gd_ss, gd_rs,
-    dhalo_ss, dhalo_rs, pair_ss, pair_rs, chip_ss, chip_rs, row_ss, row_rs, fin_ss, fin_rs,
+    dhalo_ss, dhalo_rs, paira_ss, paira_rs, pairb_ss, pairb_rs, one_a_ss, one_a_rs,
+    one_b_ss, one_b_rs, two_a_ss, two_a_rs, two_b_ss, two_b_rs, fin_ss, fin_rs,
 ):
-    n, nz, tap_rows = dims
+    n, nz, slots_a, slots_b = dims
+    loads = [
+        pltpu.make_async_copy(src, dst, load_sems.at[i])
+        for i, (src, dst) in enumerate(
+            (
+                (decay_hbm, decay), (frames_hbm, frames), (cotangent_hbm, cotangent),
+                (kernel_hbm, kernel), (start_hbm, start_state), (readout_hbm, readout),
+                (feedthrough_hbm, feedthrough),
+            )
+        )
+    ]
+    for load in loads:
+        load.start()
     frames_here, rows, width, channels = frames.shape
     state_width = kernel.shape[1]
     band_cells = rows * width
@@ -89,13 +104,9 @@
         )
 
     own_decay[...] = jnp.zeros_like(own_decay)
+    loads[0].wait()
     own_decay[0:frames_here, :] = decay[...]
     all_decay[me] = own_decay[...]
-    for s in range(n):
-        cot_send[s] = jnp.concatenate(
-            [cotangent[f, s * share : (s + 1) * share, :] for f in range(frames_here)], axis=0
-        )
-    cot_recv[me] = cot_send[me]
     pl.semaphore_wait(barrier, (n - 1) + (nz - 1))
 
     def edge_copies(src, dst, ss, rs):
@@ -139,7 +150,14 @@
             else:
                 down.wait_send()
 
-    edge_start(frames, halo, halo_ss, halo_rs)
+    edge_start(frames_hbm, halo, halo_ss, halo_rs)
+    loads[1].wait()
+    loads[2].wait()
+    for s in range(n):
+        cot_send[s] = jnp.concatenate(
+            [cotangent[f, s * share : (s + 1) * share, :] for f in range(frames_here)], axis=0
+        )
+    cot_recv[me] = cot_send[me]
 
     def over_tm(src_of, dst, ss, rs):
         copies = []
@@ -158,10 +176,11 @@
     for f in range(frames_here):
         for r in range(rows):
             place(taps, f, r + 1, frames[f, r], rows, width)
-    edge_wait(frames, halo, halo_ss, halo_rs, True)
+    edge_wait(frames_hbm, halo, halo_ss, halo_rs, True)
     for f in range(frames_here):
         place(taps, f, 0, halo[0, f], rows, width)
         place(taps, f, rows + 1, halo[1, f], rows, width)
+    loads[3].wait()
     driven[...] = jnp.dot(taps[...], kernel[...], preferred_element_type=F32)
     for s in range(n):
         drv_send[s] = jnp.concatenate(
@@ -178,9 +197,9 @@
 
     for k in range(9):
         taps_t[pl.ds(k * channels, channels), :] = taps[:, pl.ds(k * channels, channels)].T
-        kernel_t[pl.ds(k * state_width, state_width), :] = kernel[
-            pl.ds((8 - k) * channels, channels), :
-        ].T
+
+    for load in loads[4:]:
+        load.wait()
 
     for copy in dec_copies + drv_copies:
         copy.wait_recv()
@@ -221,15 +240,23 @@
     gd_recv[me] = gd_send[me]
 
     rows_here = channels // nz
-    block = tap_rows * rows_here // chips
+    block_a = slots_a * rows_here // chips
+    block_b = slots_b * rows_here // chips
+    taps_a = min(slots_a, 9)
+    in_a = {k: i for i, k in enumerate(range(9 - taps_a, 9))}
+    in_b = {k: i for i, k in enumerate([9] + [k for k in range(9) if k not in in_a])}
 
     def keep(k, product):
         rounded = product.astype(BF16)
+        part, slot, block = (
+            (grads_a, in_a[k], block_a) if k in in_a else (grads_b, in_b[k], block_b)
+        )
         for z in range(nz):
-            for j, offset, at, length in pieces(k * rows_here, rows_here, block):
+            for j, offset, at, length in pieces(slot * rows_here, rows_here, block):
                 begin = z * rows_here + at
+                place_at = (j, z) if k in in_a else (z, j)
                 for h in range(2):
-                    grads[h, j, z, pl.ds(offset, length), :] = rounded[
+                    part[(h, *place_at, pl.ds(offset, length), slice(None))] = rounded[
                         begin : begin + length, h * half : (h + 1) * half
                     ]
 
@@ -239,8 +266,24 @@
             slopes[...], flat_states, (((0,), (0,)), ((), ())), preferred_element_type=F32
         ),
     )
-    for k in range(10, tap_rows):
-        keep(k, jnp.zeros((channels, state_width), F32))
+    for part, slots, used, block in (
+        (grads_a, slots_a, len(in_a), block_a),
+        (grads_b, slots_b, len(in_b), block_b),
+    ):
+        if used < slots:
+            for j, offset, _, length in pieces(
+                used * rows_here, (slots - used) * rows_here, block
+            ):
+                for h in range(2):
+                    for z in range(nz):
+                        place_at = (j, z) if part is grads_a else (z, j)
+                        part[(h, *place_at, pl.ds(offset, length), slice(None))] = jnp.zeros(
+                            (length, half), BF16
+                        )
+    for k in range(9):
+        kernel_t[pl.ds(k * state_width, state_width), :] = kernel[
+            pl.ds((8 - k) * channels, channels), :
+        ].T
     for copy in gd_copies:
         copy.wait_recv()
     for f in range(frames_here):
@@ -253,7 +296,7 @@
         )
     edge_start(drive, drive_halo, dhalo_ss, dhalo_rs)
     flat_drive = drive[...].reshape(frames_here * band_cells, state_width)
-    for k in range(9):
+    def tap_gradient(k):
         keep(
             k,
             jnp.dot(
@@ -261,35 +304,60 @@
             ),
         )
 
-    pair_copies = []
-    for d in list(range(1, chips)) + [0]:
-        j = lax.rem(chip + d, chips)
-        pair_copies.append(
-            remote(
-                grads.at[1 - core, j], pair_recv.at[j], pair_ss.at[d], pair_rs.at[d],
-                {"tm": me + 1 - 2 * core},
+    def over_pair(grads, pair, own, count, ss, rs):
+        copies = []
+        for d in list(range(1, count)) + [0]:
+            at = lax.rem(own + d, count)
+            copies.append(
+                remote(
+                    grads.at[1 - core, at], pair.at[at], ss.at[d], rs.at[d],
+                    {"tm": me + 1 - 2 * core},
+                )
             )
-        )
-        pair_copies[-1].start()
+            copies[-1].start()
+        return copies
+
+    for k in range(9):
+        if k in in_b:
+            tap_gradient(k)
+    pair_b_copies = over_pair(grads_b, pair_b, band, nz, pairb_ss, pairb_rs)
+    for k in range(9):
+        if k in in_a:
+            tap_gradient(k)
+    pair_a_copies = over_pair(grads_a, pair_a, chip, chips, paira_ss, paira_rs)
+
+    def first_sum(pair_copies, grads, pair, own, count, send, recv, ss, rs, where, total):
+        copies = []
+        for d in range(1, count):
+            at = lax.rem(own + d, count)
+            pair_copies[d - 1].wait_recv()
+            send[d - 1] = (grads[core, at].astype(F32) + pair[at].astype(F32)).astype(BF16)
+            copies.append(
+                remote(send.at[d - 1], recv.at[d - 1], ss.at[d - 1], rs.at[d - 1], where(at))
+            )
+            copies[-1].start()
+        pair_copies[-1].wait_recv()
+        total[...] = grads[core, own].astype(F32) + pair[own].astype(F32)
+        return copies
+
+    def to_chip(j):
+        return {"tm": 2 * j + core}
+
+    def to_band(z):
+        return {"row": z}
+
+    one_b = first_sum(
+        pair_b_copies, grads_b, pair_b, band, nz, send1_b, recv1_b, one_b_ss, one_b_rs,
+        to_band, total_b,
+    )
+    one_a = first_sum(
+        pair_a_copies, grads_a, pair_a, chip, chips, send1_a, recv1_a, one_a_ss, one_a_rs,
+        to_chip, total_a,
+    )
+
     for f in range(frames_here):
         for r in range(rows):
             place(drive_taps, f, r + 1, drive[f, r], rows, width)
-
-    chip_copies = []
-    for d in range(1, chips):
-        j = lax.rem(chip + d, chips)
-        pair_copies[d - 1].wait_recv()
-        chip_send[d - 1] = (grads[core, j].astype(F32) + pair_recv[j].astype(F32)).astype(BF16)
-        chip_copies.append(
-            remote(
-                chip_send.at[d - 1], chip_recv.at[d - 1], chip_ss.at[d - 1], chip_rs.at[d - 1],
-                {"tm": 2 * j + core},
-            )
-        )
-        chip_copies[-1].start()
-    pair_copies[-1].wait_recv()
-    total[...] = grads[core, chip].astype(F32) + pair_recv[chip].astype(F32)
-
     edge_wait(drive, drive_halo, dhalo_ss, dhalo_rs, True)
     for f in range(frames_here):
         place(drive_taps, f, 0, drive_halo[0, f], rows, width)
@@ -301,47 +369,59 @@
             + feedthrough[...] * cotangent[f].astype(F32)
         ).astype(BF16)
 
-    for copy in chip_copies:
-        copy.wait_recv()
-    summed = total[...]
-    for d in range(1, chips):
-        summed = summed + chip_recv[d - 1].astype(F32)
-    total[...] = summed
-    row_send[...] = summed.astype(BF16)
-
-    row_copies = []
-    for d in range(1, nz):
-        z = lax.rem(band + d, nz)
-        row_copies.append(
-            remote(
-                row_send.at[z], row_recv.at[d - 1], row_ss.at[d - 1], row_rs.at[d - 1], {"row": z}
+    def second_sum(one, recv1, total, own, count, send, recv, ss, rs, where):
+        summed = total[...]
+        for i, copy in enumerate(one):
+            copy.wait_recv()
+            summed = summed + recv1[i].astype(F32)
+        total[...] = summed
+        send[...] = summed.astype(BF16)
+        copies = []
+        for d in range(1, count):
+            at = lax.rem(own + d, count)
+            copies.append(
+                remote(send.at[at], recv.at[d - 1], ss.at[d - 1], rs.at[d - 1], where(at))
             )
-        )
-        row_copies[-1].start()
-    for copy in row_copies:
-        copy.wait_recv()
-    mine = total[band]
-    for d in range(1, nz):
-        mine = mine + row_recv[d - 1].astype(F32)
-    final[me] = mine.astype(BF16)
+            copies[-1].start()
+        return copies
+
+    two_b = second_sum(
+        one_b, recv1_b, total_b, chip, chips, send2_b, recv2_b, two_b_ss, two_b_rs, to_chip
+    )
+    two_a = second_sum(
+        one_a, recv1_a, total_a, band, nz, send2_a, recv2_a, two_a_ss, two_a_rs, to_band
+    )
+    for two, recv2, total, own, begin, block in (
+        (two_b, recv2_b, total_b, chip, block_a, block_b),
+        (two_a, recv2_a, total_a, band, 0, block_a),
+    ):
+        mine = total[own]
+        for i, copy in enumerate(two):
+            copy.wait_recv()
+            mine = mine + recv2[i].astype(F32)
+        final[me, pl.ds(begin, block), :] = mine.astype(BF16)
 
     fin_copies = over_tm(lambda to: final.at[me], final, fin_ss, fin_rs)
     for copy in fin_copies:
         copy.start()
-    for copies in (dec_copies, cot_copies, drv_copies, gd_copies, pair_copies, chip_copies):
+    for copies in (
+        dec_copies, cot_copies, drv_copies, gd_copies, pair_a_copies, pair_b_copies, one_a, one_b,
+        two_a, two_b,
+    ):
         for copy in copies:
             copy.wait_send()
-    edge_wait(frames, halo, halo_ss, halo_rs, False)
+    edge_wait(frames_hbm, halo, halo_ss, halo_rs, False)
     edge_wait(drive, drive_halo, dhalo_ss, dhalo_rs, False)
-    for copy in row_copies:
-        copy.wait_send()
     for copy in fin_copies:
         copy.wait_recv()
     scaling = 1.0 / math.sqrt(frames_here * band_cells * n * nz)
     for k in range(10):
-        for j, offset, at, length in pieces(k * rows_here, rows_here, block):
+        slot, block, begin = (
+            (in_a[k], block_a, 0) if k in in_a else (in_b[k], block_b, block_a)
+        )
+        for j, offset, at, length in pieces(slot * rows_here, rows_here, block):
             for h in range(2):
-                value = final[2 * j + h, pl.ds(offset, length), :].astype(F32) * scaling
+                value = final[2 * j + h, pl.ds(begin + offset, length), :].astype(F32) * scaling
                 lanes = pl.ds(h * half, half)
                 if k < 9:
                     grad_kernel[k, pl.ds(at, length), lanes] = value
@@ -359,16 +439,25 @@
     chips = n // 2
     rows_here = channels // nz
     half = state_width // 2
-    tap_rows = 10
-    while tap_rows * rows_here % (16 * chips):
-        tap_rows += 1
-    block = tap_rows * rows_here // chips
+    step = 16 * chips // math.gcd(rows_here, 16 * chips)
+    slots_a = -(-7 // step) * step
+    slots_b = -(-max(10 - slots_a, 1) // step) * step
+    block_a = slots_a * rows_here // chips
+    block_b = slots_b * rows_here // chips
     mixed = frames_here * share
     vmem = pltpu.VMEM
     dma = pltpu.SemaphoreType.DMA
     whole = pl.BlockSpec(memory_space=pltpu.VMEM)
     every = frames_here * cells
     scratch = [
+        vmem(frames_in.shape, BF16),
+        vmem((frames_here, cells, channels), BF16),
+        vmem((9 * channels, state_width), BF16),
+        vmem(readout.shape, BF16),
+        vmem((1, channels), F32),
+        vmem(decay_rate.shape, F32),
+        vmem((cells, state_width), F32),
+        dma((7,)),
         vmem((every, 9 * channels), BF16),
         vmem((9 * channels, every), BF16),
         vmem((9 * state_width, channels), BF16),
@@ -388,29 +477,38 @@
         vmem((n, mixed, state_width), BF16),
         vmem((n, mixed, state_width), BF16),
         vmem((frames_here, rows, width, state_width), BF16),
-        vmem((2, chips, nz, block, half), BF16),
-        vmem((chips, nz, block, half), BF16),
-        vmem((chips - 1, nz, block, half), BF16),
-        vmem((chips - 1, nz, block, half), BF16),
-        vmem((nz, block, half), F32),
-        vmem((nz, block, half), BF16),
-        vmem((nz - 1, block, half), BF16),
-        vmem((n, block, half), BF16),
+        vmem((2, chips, nz, block_a, half), BF16),
+        vmem((2, nz, chips, block_b, half), BF16),
+        vmem((chips, nz, block_a, half), BF16),
+        vmem((nz, chips, block_b, half), BF16),
+        vmem((chips - 1, nz, block_a, half), BF16),
+        vmem((nz - 1, chips, block_b, half), BF16),
+        vmem((chips - 1, nz, block_a, half), BF16),
+        vmem((nz - 1, chips, block_b, half), BF16),
+        vmem((nz, block_a, half), F32),
+        vmem((chips, block_b, half), F32),
+        vmem((nz, block_a, half), BF16),
+        vmem((chips, block_b, half), BF16),
+        vmem((nz - 1, block_a, half), BF16),
+        vmem((chips - 1, block_b, half), BF16),
+        vmem((n, block_a + block_b, half), BF16),
     ]
-    for count in (2, n - 1, n - 1, n - 1, n - 1, 2, chips, chips - 1, nz - 1, n - 1):
+    counts = (2, n - 1, n - 1, n - 1, n - 1, 2)
+    counts += (chips, nz, chips - 1, nz - 1, nz - 1, chips - 1, n - 1)
+    for count in counts:
         scratch += [dma((count,)), dma((count,))]
     spread, kernel_part, readout_part = pl.pallas_call(
-        functools.partial(fused, (n, nz, tap_rows)),
+        functools.partial(fused, (n, nz, slots_a, slots_b)),
         out_shape=(
             jax.ShapeDtypeStruct((frames_here, cells, channels), BF16),
             jax.ShapeDtypeStruct((9, rows_here, state_width), F32),
             jax.ShapeDtypeStruct((rows_here, state_width), F32),
         ),
-        in_specs=[whole] * 7,
+        in_specs=[pl.BlockSpec(memory_space=pltpu.HBM)] * 7,
         out_specs=(whole, whole, whole),
         scratch_shapes=scratch,
         compiler_params=pltpu.CompilerParams(
-            collective_id=0, has_side_effects=True, vmem_limit_bytes=48 * 1024 * 1024
+            collective_id=0, has_side_effects=True, vmem_limit_bytes=60 * 1024 * 1024
         ),
         cost_estimate=pl.CostEstimate(
             flops=2 * every * channels * state_width * 30,

time: 52.2 us -> 45.6 us (0.87)
  local copies, waits for them, and re-layouts: 8.52 us -> 4.25 us
  Pallas kernels: 42.7 us -> 40.5 us
    unnamed x17 -> x5, local copies, waits for them, and re-layouts: 8.52 us -> 4.25 us
    pallas_call x1, Pallas kernels: 42.7 us -> 40.5 us  [local(): pl.pallas_call(functools.partial(fused, (n, nz, slots_a, slots_b)), out_s...]
where the time goes in v2:
time: 45.6 us; the launch traced here: 45.4 us
  Pallas kernels  40.5 us (89%)
  local copies, waits for them, and re-layouts  4.25 us (9%)
  between operations  0.65 us (1%)
    pallas_call x1, Pallas kernels, local(): pl.pallas_call(functools.partial(fused, (n, nz, slots_a, slots_b)), out_s...  40.5 us
    unnamed x5, local copies, waits for them, and re-layouts  4.25 us

profile of v2, /device:TPU:0, one launch (start us, length us, event | category | flops | bytes accessed | tf_op | source)
XLA Modules:
  0.0 45.4 jit_solution(17255268895880639015)
XLA Ops:
  0.6 40.5 %conv_s5_backward.1 = (bf16[2,256,256]{2,1,0:T(8,128)(2,1)}, f32[9,64,256]{2,1,0:T(8,128)}, f32[64,256]{1,0:T(8,128)}) custom-call(bf16[2,4,64,256]{3,2,1,0:T(8,128)(2,1)} %frames_hbm.1, bf16[2,256,256]{2,1,0:T(8,128)(2,1)} %bitcast.9, bf16[2304,256]{1,0:T(8,128)(2,1)} %bitcast.8, bf16[256,256]{1,0:T(8,128)(2,1)} %readout_hbm.1, f32[1,256]{1,0:T(1,128)} %bitcast.11, ...), custom_call_target="tpu_custom_call" | custom-call | flops 2013265920 | bytes 6291456 | tf_op jit(solution)/shard_map/conv_s5_backward/pallas_call | solution.py:500
  41.2 0.0 copy-start
  41.2 1.7 %copy.13 = bf16[2,4,64,256]{3,2,1,0:T(8,128)(2,1)} copy(bf16[2,4,64,256]{3,2,1,0:T(8,128)(2,1)} %bitcast.6) | data formatting | bytes 524288
  42.9 1.9 %copy.14 = f32[9,64,256]{2,1,0:T(8,128)} copy(f32[9,64,256]{2,1,0:T(8,128)} %get-tuple-element.13) | data formatting | bytes 1179648
  44.8 0.0 copy-done
  44.8 0.6 %copy.15 = f32[256,64]{0,1:T(8,128)} copy(f32[256,64]{0,1:T(8,128)S(1)} %bitcast.7) | data formatting | bytes 131072
Async XLA Ops:
  41.2 3.6 %copy-start = (f32[64,256]{1,0:T(8,128)S(1)}, f32[64,256]{1,0:T(8,128)}, u32[]{:S(2)}) copy-start(f32[64,256]{1,0:T(8,128)} %get-tuple-element.8) | copy-start | bytes 196612

commit v3 on v2

--- a/solution.py
+++ b/solution.py
@@ -48,22 +48,29 @@
         done += length
 
 
+def places(slots_a):
+    taps_a = min(slots_a, 9)
+    in_a = {k: i for i, k in enumerate(range(9 - taps_a, 9))}
+    in_b = {k: i for i, k in enumerate([9] + list(range(9 - taps_a)))}
+    return in_a, in_b
+
+
 def fused(
     dims,
     frames_hbm, cotangent_hbm, kernel_hbm, readout_hbm, feedthrough_hbm, decay_hbm, start_hbm,
-    grad_frames, grad_kernel, grad_readout,
+    grad_frames, gathered,
     frames, cotangent, kernel, readout, feedthrough, decay, start_state, load_sems,
     taps, taps_t, kernel_t, drive_taps,
     halo, drive_halo, own_decay, all_decay,
     cot_send, cot_recv, driven, drv_send, drv_recv,
     states_bf, slopes, pulled, gd_send, gd_recv, drive,
     grads_a, grads_b, pair_a, pair_b, send1_a, send1_b, recv1_a, recv1_b, total_a, total_b,
-    send2_a, send2_b, recv2_a, recv2_b, final,
+    send2_a, send2_b, recv2_a, recv2_b, final, spread_bf,
     halo_ss, halo_rs, dec_ss, dec_rs, cot_ss, cot_rs, drv_ss, drv_rs, gd_ss, gd_rs,
     dhalo_ss, dhalo_rs, paira_ss, paira_rs, pairb_ss, pairb_rs, one_a_ss, one_a_rs,
-    one_b_ss, one_b_rs, two_a_ss, two_a_rs, two_b_ss, two_b_rs, fin_ss, fin_rs,
+    one_b_ss, one_b_rs, two_a_ss, two_a_rs, two_b_ss, two_b_rs, fin_ss, fin_rs, sib_ss, sib_rs,
 ):
-    n, nz, slots_a, slots_b = dims
+    n, nz, slots_a, slots_b, groups = dims
     loads = [
         pltpu.make_async_copy(src, dst, load_sems.at[i])
         for i, (src, dst) in enumerate(
@@ -81,6 +88,7 @@
     band_cells = rows * width
     share = band_cells // n
     chips = n // 2
+    part_cells = share // groups
     half = state_width // 2
     me = lax.axis_index("tm")
     band = lax.axis_index("row")
@@ -153,12 +161,6 @@
     edge_start(frames_hbm, halo, halo_ss, halo_rs)
     loads[1].wait()
     loads[2].wait()
-    for s in range(n):
-        cot_send[s] = jnp.concatenate(
-            [cotangent[f, s * share : (s + 1) * share, :] for f in range(frames_here)], axis=0
-        )
-    cot_recv[me] = cot_send[me]
-
     def over_tm(src_of, dst, ss, rs):
         copies = []
         for d in range(1, n):
@@ -168,10 +170,29 @@
             )
         return copies
 
+    def cells_of(s, g):
+        begin = s * share + g * part_cells
+        return slice(begin, begin + part_cells)
+
+    for g in range(groups):
+        for s in range(n):
+            cot_send[g, s] = jnp.concatenate(
+                [cotangent[f, cells_of(s, g), :] for f in range(frames_here)], axis=0
+            )
+        cot_recv[g, me] = cot_send[g, me]
+
     dec_copies = over_tm(lambda to: own_decay, all_decay, dec_ss, dec_rs)
-    cot_copies = over_tm(lambda to: cot_send.at[to], cot_recv, cot_ss, cot_rs)
-    for copy in dec_copies + cot_copies:
+    for copy in dec_copies:
         copy.start()
+    cot_copies = []
+    for g in range(groups):
+        cot_copies.append(
+            over_tm(
+                lambda to, g=g: cot_send.at[g, to], cot_recv.at[g], cot_ss.at[g], cot_rs.at[g]
+            )
+        )
+        for copy in cot_copies[g]:
+            copy.start()
 
     for f in range(frames_here):
         for r in range(rows):
@@ -181,70 +202,78 @@
         place(taps, f, 0, halo[0, f], rows, width)
         place(taps, f, rows + 1, halo[1, f], rows, width)
     loads[3].wait()
-    driven[...] = jnp.dot(taps[...], kernel[...], preferred_element_type=F32)
-    for s in range(n):
-        drv_send[s] = jnp.concatenate(
-            [
-                driven[f * band_cells + s * share : f * band_cells + (s + 1) * share, :]
-                for f in range(frames_here)
-            ],
-            axis=0,
-        ).astype(BF16)
-    drv_copies = over_tm(lambda to: drv_send.at[to], drv_recv, drv_ss, drv_rs)
-    for copy in drv_copies:
-        copy.start()
-    drv_recv[me] = drv_send[me]
+    driven[...] = jnp.dot(taps[...], kernel[...], preferred_element_type=F32).reshape(driven.shape)
+    drv_copies = []
+    for g in range(groups):
+        for s in range(n):
+            drv_send[g, s] = jnp.concatenate(
+                [driven[f, cells_of(s, g), :] for f in range(frames_here)], axis=0
+            ).astype(BF16)
+        drv_copies.append(
+            over_tm(
+                lambda to, g=g: drv_send.at[g, to], drv_recv.at[g], drv_ss.at[g], drv_rs.at[g]
+            )
+        )
+        for copy in drv_copies[g]:
+            copy.start()
+        drv_recv[g, me] = drv_send[g, me]
 
     for k in range(9):
         taps_t[pl.ds(k * channels, channels), :] = taps[:, pl.ds(k * channels, channels)].T
 
-    for load in loads[4:]:
+    for load in loads[4:7]:
         load.wait()
 
-    for copy in dec_copies + drv_copies:
+    for copy in dec_copies:
         copy.wait_recv()
-    state = start_state[pl.ds(pl.multiple_of(me * share, share), share), :]
-    for s in range(n):
-        arrived = drv_recv[s].astype(F32)
-        kept = []
-        for f in range(frames_here):
-            rate = all_decay[s, f : f + 1, :]
-            gain = jnp.sqrt(1.0 - rate * rate)
-            state = rate * state + gain * arrived[f * share : (f + 1) * share]
-            kept.append(state)
-        states_bf[s] = jnp.concatenate(kept, axis=0).astype(BF16)
-    for copy in cot_copies:
-        copy.wait_recv()
-    flat = n * frames_here * share
-    flat_states = states_bf[...].reshape(flat, state_width)
-    mixture = jnp.dot(flat_states, readout[...], preferred_element_type=F32)
-    slopes[...] = (
-        cot_recv[...].reshape(flat, channels).astype(F32) * gelu_slope(mixture)
-    ).astype(BF16)
-    pulled[...] = lax.dot_general(
-        slopes[...], readout[...], (((1,), (1,)), ((), ())), preferred_element_type=F32
-    )
-    adjoint = jnp.zeros((share, state_width), F32)
-    rate = jnp.zeros((1, state_width), F32)
-    for s in reversed(range(n)):
-        kept = []
-        for f in reversed(range(frames_here)):
-            at = (s * frames_here + f) * share
-            adjoint = pulled[at : at + share, :] + rate * adjoint
-            rate = all_decay[s, f : f + 1, :]
-            kept.append(jnp.sqrt(1.0 - rate * rate) * adjoint)
-        gd_send[s] = jnp.concatenate(kept[::-1], axis=0).astype(BF16)
-    gd_copies = over_tm(lambda to: gd_send.at[to], gd_recv, gd_ss, gd_rs)
-    for copy in gd_copies:
-        copy.start()
-    gd_recv[me] = gd_send[me]
+    flat = n * frames_here * part_cells
+    gd_copies = []
+    for g in range(groups):
+        for copy in drv_copies[g]:
+            copy.wait_recv()
+        begin = pl.multiple_of(me * share + g * part_cells, part_cells)
+        state = start_state[pl.ds(begin, part_cells), :]
+        for s in range(n):
+            arrived = drv_recv[g, s].astype(F32)
+            kept = []
+            for f in range(frames_here):
+                rate = all_decay[s, f : f + 1, :]
+                gain = jnp.sqrt(1.0 - rate * rate)
+                state = rate * state + gain * arrived[f * part_cells : (f + 1) * part_cells]
+                kept.append(state)
+            states_bf[g, s] = jnp.concatenate(kept, axis=0).astype(BF16)
+        for copy in cot_copies[g]:
+            copy.wait_recv()
+        mixture = jnp.dot(
+            states_bf[g].reshape(flat, state_width), readout[...], preferred_element_type=F32
+        )
+        slopes[g] = (
+            cot_recv[g].reshape(flat, channels).astype(F32) * gelu_slope(mixture)
+        ).astype(BF16)
+        pulled[...] = lax.dot_general(
+            slopes[g], readout[...], (((1,), (1,)), ((), ())), preferred_element_type=F32
+        )
+        adjoint = jnp.zeros((part_cells, state_width), F32)
+        rate = jnp.zeros((1, state_width), F32)
+        for s in reversed(range(n)):
+            kept = []
+            for f in reversed(range(frames_here)):
+                at = (s * frames_here + f) * part_cells
+                adjoint = pulled[at : at + part_cells, :] + rate * adjoint
+                rate = all_decay[s, f : f + 1, :]
+                kept.append(jnp.sqrt(1.0 - rate * rate) * adjoint)
+            gd_send[g, s] = jnp.concatenate(kept[::-1], axis=0).astype(BF16)
+        gd_copies.append(
+            over_tm(lambda to, g=g: gd_send.at[g, to], gd_recv.at[g], gd_ss.at[g], gd_rs.at[g])
+        )
+        for copy in gd_copies[g]:
+            copy.start()
+        gd_recv[g, me] = gd_send[g, me]
 
     rows_here = channels // nz
     block_a = slots_a * rows_here // chips
     block_b = slots_b * rows_here // chips
-    taps_a = min(slots_a, 9)
-    in_a = {k: i for i, k in enumerate(range(9 - taps_a, 9))}
-    in_b = {k: i for i, k in enumerate([9] + [k for k in range(9) if k not in in_a])}
+    in_a, in_b = places(slots_a)
 
     def keep(k, product):
         rounded = product.astype(BF16)
@@ -263,7 +292,9 @@
     keep(
         9,
         lax.dot_general(
-            slopes[...], flat_states, (((0,), (0,)), ((), ())), preferred_element_type=F32
+            slopes[...].reshape(groups * flat, channels),
+            states_bf[...].reshape(groups * flat, state_width),
+            (((0,), (0,)), ((), ())), preferred_element_type=F32
         ),
     )
     for part, slots, used, block in (
@@ -284,12 +315,18 @@
         kernel_t[pl.ds(k * state_width, state_width), :] = kernel[
             pl.ds((8 - k) * channels, channels), :
         ].T
-    for copy in gd_copies:
-        copy.wait_recv()
+    for copies in gd_copies:
+        for copy in copies:
+            copy.wait_recv()
     for f in range(frames_here):
         drive[f] = (
             jnp.concatenate(
-                [gd_recv[s, f * share : (f + 1) * share, :].astype(F32) for s in range(n)], axis=0
+                [
+                    gd_recv[g, s, f * part_cells : (f + 1) * part_cells, :].astype(F32)
+                    for s in range(n)
+                    for g in range(groups)
+                ],
+                axis=0,
             )
             .astype(BF16)
             .reshape(rows, width, state_width)
@@ -364,10 +401,13 @@
         place(drive_taps, f, rows + 1, drive_halo[1, f], rows, width)
     spread = jnp.dot(drive_taps[...], kernel_t[...], preferred_element_type=F32)
     for f in range(frames_here):
-        grad_frames[f] = (
+        spread_bf[f] = (
             spread[f * band_cells : (f + 1) * band_cells]
             + feedthrough[...] * cotangent[f].astype(F32)
         ).astype(BF16)
+
+    out_copies = [pltpu.make_async_copy(spread_bf, grad_frames, load_sems.at[7])]
+    out_copies[0].start()
 
     def second_sum(one, recv1, total, own, count, send, recv, ss, rs, where):
         summed = total[...]
@@ -401,34 +441,75 @@
             mine = mine + recv2[i].astype(F32)
         final[me, pl.ds(begin, block), :] = mine.astype(BF16)
 
-    fin_copies = over_tm(lambda to: final.at[me], final, fin_ss, fin_rs)
+    sibling = {"tm": me + 1 - 2 * core}
+    fin_copies = []
+    for d in range(1, chips):
+        j = lax.rem(chip + d, chips)
+        fin_copies.append(
+            remote(final.at[me], final.at[me], fin_ss.at[d - 1], fin_rs.at[d - 1], to_chip(j))
+        )
+    sib_copies = []
+    for d in range(chips):
+        at = 2 * lax.rem(chip - d + chips, chips) + core
+        sib_copies.append(
+            remote(final.at[at], final.at[at], sib_ss.at[d], sib_rs.at[d], sibling)
+        )
     for copy in fin_copies:
         copy.start()
-    for copies in (
-        dec_copies, cot_copies, drv_copies, gd_copies, pair_a_copies, pair_b_copies, one_a, one_b,
-        two_a, two_b,
-    ):
-        for copy in copies:
-            copy.wait_send()
+    sib_copies[0].start()
+    flat_copies = dec_copies
+    for copies in cot_copies + drv_copies + gd_copies:
+        flat_copies = flat_copies + copies
+    for copies in (pair_a_copies, pair_b_copies, one_a, one_b, two_a, two_b):
+        flat_copies = flat_copies + copies
+    for copy in flat_copies:
+        copy.wait_send()
     edge_wait(frames_hbm, halo, halo_ss, halo_rs, False)
     edge_wait(drive, drive_halo, dhalo_ss, dhalo_rs, False)
-    for copy in fin_copies:
+    for d in range(1, chips):
+        fin_copies[d - 1].wait_recv()
+        sib_copies[d].start()
+    for copy in sib_copies:
         copy.wait_recv()
-    scaling = 1.0 / math.sqrt(frames_here * band_cells * n * nz)
+    out_copies.append(pltpu.make_async_copy(final, gathered, load_sems.at[8]))
+    out_copies[1].start()
+    for copy in fin_copies + sib_copies:
+        copy.wait_send()
+    for copy in out_copies:
+        copy.wait()
+
+
+def finish(
+    dims,
+    spread, gathered, grad_frames, grad_kernel, grad_readout,
+    final, scaled, scaled_readout, sems,
+):
+    chips, slots_a, block_a, block_b, in_a, in_b, scaling = dims
+    rows_here, state_width = scaled_readout.shape
+    half = state_width // 2
+    through = pltpu.make_async_copy(spread, grad_frames, sems.at[0])
+    load = pltpu.make_async_copy(gathered, final, sems.at[1])
+    load.start()
+    through.start()
+    load.wait()
     for k in range(10):
-        slot, block, begin = (
-            (in_a[k], block_a, 0) if k in in_a else (in_b[k], block_b, block_a)
-        )
+        slot, block, begin = (in_a[k], block_a, 0) if k in in_a else (in_b[k], block_b, block_a)
         for j, offset, at, length in pieces(slot * rows_here, rows_here, block):
             for h in range(2):
                 value = final[2 * j + h, pl.ds(begin + offset, length), :].astype(F32) * scaling
                 lanes = pl.ds(h * half, half)
                 if k < 9:
-                    grad_kernel[k, pl.ds(at, length), lanes] = value
+                    scaled[k, pl.ds(at, length), lanes] = value
                 else:
-                    grad_readout[pl.ds(at, length), lanes] = value
-    for copy in fin_copies:
-        copy.wait_send()
+                    scaled_readout[pl.ds(at, length), lanes] = value
+    stores = [
+        pltpu.make_async_copy(scaled, grad_kernel, sems.at[2]),
+        pltpu.make_async_copy(scaled_readout, grad_readout, sems.at[3]),
+    ]
+    for store in stores:
+        store.start()
+    for copy in stores + [through]:
+        copy.wait()
 
 
 def local(n, nz, frames_in, cotangent, kernel, readout, feedthrough, decay_rate, start_state):
@@ -444,10 +525,13 @@
     slots_b = -(-max(10 - slots_a, 1) // step) * step
     block_a = slots_a * rows_here // chips
     block_b = slots_b * rows_here // chips
-    mixed = frames_here * share
+    groups = 2 if frames_here * share // 2 % 16 == 0 and share % 16 == 0 else 1
+    mixed = frames_here * share // groups
+    scaling = 1.0 / math.sqrt(frames_here * cells * n * nz)
     vmem = pltpu.VMEM
     dma = pltpu.SemaphoreType.DMA
-    whole = pl.BlockSpec(memory_space=pltpu.VMEM)
+    any_space = pl.BlockSpec(memory_space=pl.ANY)
+    hbm = pl.BlockSpec(memory_space=pltpu.HBM)
     every = frames_here * cells
     scratch = [
         vmem(frames_in.shape, BF16),
@@ -457,7 +541,7 @@
         vmem((1, channels), F32),
         vmem(decay_rate.shape, F32),
         vmem((cells, state_width), F32),
-        dma((7,)),
+        dma((9,)),
         vmem((every, 9 * channels), BF16),
         vmem((9 * channels, every), BF16),
         vmem((9 * state_width, channels), BF16),
@@ -466,16 +550,16 @@
         vmem((2, frames_here, width, state_width), BF16),
         vmem((8, state_width), F32),
         vmem((n, 8, state_width), F32),
-        vmem((n, mixed, channels), BF16),
-        vmem((n, mixed, channels), BF16),
-        vmem((every, state_width), F32),
-        vmem((n, mixed, state_width), BF16),
-        vmem((n, mixed, state_width), BF16),
-        vmem((n, mixed, state_width), BF16),
-        vmem((n * mixed, channels), BF16),
+        vmem((groups, n, mixed, channels), BF16),
+        vmem((groups, n, mixed, channels), BF16),
+        vmem((frames_here, cells, state_width), F32),
+        vmem((groups, n, mixed, state_width), BF16),
+        vmem((groups, n, mixed, state_width), BF16),
+        vmem((groups, n, mixed, state_width), BF16),
+        vmem((groups, n * mixed, channels), BF16),
         vmem((n * mixed, state_width), F32),
-        vmem((n, mixed, state_width), BF16),
-        vmem((n, mixed, state_width), BF16),
+        vmem((groups, n, mixed, state_width), BF16),
+        vmem((groups, n, mixed, state_width), BF16),
         vmem((frames_here, rows, width, state_width), BF16),
         vmem((2, chips, nz, block_a, half), BF16),
         vmem((2, nz, chips, block_b, half), BF16),
@@ -492,20 +576,20 @@
         vmem((nz - 1, block_a, half), BF16),
         vmem((chips - 1, block_b, half), BF16),
         vmem((n, block_a + block_b, half), BF16),
+        vmem((frames_here, cells, channels), BF16),
     ]
-    counts = (2, n - 1, n - 1, n - 1, n - 1, 2)
-    counts += (chips, nz, chips - 1, nz - 1, nz - 1, chips - 1, n - 1)
-    for count in counts:
-        scratch += [dma((count,)), dma((count,))]
-    spread, kernel_part, readout_part = pl.pallas_call(
-        functools.partial(fused, (n, nz, slots_a, slots_b)),
+    counts = ((2,), (n - 1,), (groups, n - 1), (groups, n - 1), (groups, n - 1), (2,))
+    counts += ((chips,), (nz,), (chips - 1,), (nz - 1,), (nz - 1,), (chips - 1,))
+    for count in counts + ((chips - 1,), (chips,)):
+        scratch += [dma(count), dma(count)]
+    spread, gathered = pl.pallas_call(
+        functools.partial(fused, (n, nz, slots_a, slots_b, groups)),
         out_shape=(
             jax.ShapeDtypeStruct((frames_here, cells, channels), BF16),
-            jax.ShapeDtypeStruct((9, rows_here, state_width), F32),
-            jax.ShapeDtypeStruct((rows_here, state_width), F32),
+            jax.ShapeDtypeStruct((n, block_a + block_b, half), BF16),
         ),
-        in_specs=[pl.BlockSpec(memory_space=pltpu.HBM)] * 7,
-        out_specs=(whole, whole, whole),
+        in_specs=[hbm] * 7,
+        out_specs=(hbm, hbm),
         scratch_shapes=scratch,
         compiler_params=pltpu.CompilerParams(
             collective_id=0, has_side_effects=True, vmem_limit_bytes=60 * 1024 * 1024
@@ -525,6 +609,25 @@
         decay_rate,
         start_state.reshape(cells, state_width),
     )
+    in_a, in_b = places(slots_a)
+    spread, kernel_part, readout_part = pl.pallas_call(
+        functools.partial(finish, (chips, slots_a, block_a, block_b, in_a, in_b, scaling)),
+        out_shape=(
+            jax.ShapeDtypeStruct((frames_here, cells, channels), BF16),
+            jax.ShapeDtypeStruct((9, rows_here, state_width), F32),
+            jax.ShapeDtypeStruct((rows_here, state_width), F32),
+        ),
+        in_specs=[any_space] * 2,
+        out_specs=(any_space,) * 3,
+        scratch_shapes=[
+            vmem((n, block_a + block_b, half), BF16),
+            vmem((9, rows_here, state_width), F32),
+            vmem((rows_here, state_width), F32),
+            dma((4,)),
+        ],
+        compiler_params=pltpu.CompilerParams(vmem_limit_bytes=60 * 1024 * 1024),
+        name="write_outputs",
+    )(spread, gathered)
     return (spread.reshape(frames_in.shape), kernel_part, readout_part.T)
 
 

time: 45.6 us -> 50.3 us (1.10); the launches traced: 45.4 us -> 49.5 us
  Pallas kernels: 40.5 us -> 48.9 us
  local copies, waits for them, and re-layouts: 4.25 us -> 0 us
    pallas_call x1 -> x2, Pallas kernels: 40.5 us -> 48.9 us  [the longest x1 39.8 us: local(): pl.pallas_call(functools.partial(fused, (n, nz, slots_a, slots_b, groups)...]
    unnamed x5 -> x0, local copies, waits for them, and re-layouts: 4.25 us -> none
where the time goes in v3:
time: 50.3 us; the launch traced here: 49.5 us
  Pallas kernels  48.9 us (97%)
  between operations  0.64 us (1%)
    pallas_call x1, Pallas kernels, local(): pl.pallas_call(functools.partial(fused, (n, nz, slots_a, slots_b, groups)...  39.8 us
    pallas_call x1, Pallas kernels, local(): pl.pallas_call(functools.partial(finish, (chips, slots_a, block_a, block_...  9.08 us

profile of v3, /device:TPU:0, one launch (start us, length us, event | category | flops | bytes accessed | tf_op | source)
XLA Modules:
  0.0 49.5 jit_solution(13398701940532085323)
XLA Ops:
  0.6 39.8 %conv_s5_backward.1 = (bf16[2,256,256]{2,1,0:T(8,128)(2,1)}, bf16[8,160,128]{2,1,0:T(8,128)(2,1)}) custom-call(bf16[2,4,64,256]{3,2,1,0:T(8,128)(2,1)} %frames_hbm.1, bf16[2,256,256]{2,1,0:T(8,128)(2,1)} %bitcast.7, bf16[2304,256]{1,0:T(8,128)(2,1)} %bitcast.6, bf16[256,256]{1,0:T(8,128)(2,1)} %readout_hbm.1, f32[1,256]{1,0:T(1,128)} %bitcast.11, ...), custom_call_target="tpu_custom_call" | custom-call | flops 2013265920 | bytes 6291456 | tf_op jit(solution)/shard_map/conv_s5_backward/pallas_call | solution.py:585
  40.4 9.1 %write_outputs.1 = (bf16[2,256,256]{2,1,0:T(8,128)(2,1)}, f32[9,64,256]{2,1,0:T(8,128)}, f32[64,256]{1,0:T(8,128)}) custom-call(bf16[2,256,256]{2,1,0:T(8,128)(2,1)} %get-tuple-element.8.spread, bf16[8,160,128]{2,1,0:T(8,128)(2,1)} %get-tuple-element.9.gathered), custom_call_target="tpu_custom_call" | custom-call | tf_op jit(solution)/shard_map/write_outputs/pallas_call | solution.py:613

commit v4 on v3

--- a/solution.py
+++ b/solution.py
@@ -58,14 +58,14 @@
 def fused(
     dims,
     frames_hbm, cotangent_hbm, kernel_hbm, readout_hbm, feedthrough_hbm, decay_hbm, start_hbm,
-    grad_frames, gathered,
+    grad_frames, final,
     frames, cotangent, kernel, readout, feedthrough, decay, start_state, load_sems,
-    taps, taps_t, kernel_t, drive_taps,
+    taps, taps_t, drive_taps,
     halo, drive_halo, own_decay, all_decay,
     cot_send, cot_recv, driven, drv_send, drv_recv,
     states_bf, slopes, pulled, gd_send, gd_recv, drive,
     grads_a, grads_b, pair_a, pair_b, send1_a, send1_b, recv1_a, recv1_b, total_a, total_b,
-    send2_a, send2_b, recv2_a, recv2_b, final, spread_bf,
+    send2_a, send2_b, recv2_a, recv2_b,
     halo_ss, halo_rs, dec_ss, dec_rs, cot_ss, cot_rs, drv_ss, drv_rs, gd_ss, gd_rs,
     dhalo_ss, dhalo_rs, paira_ss, paira_rs, pairb_ss, pairb_rs, one_a_ss, one_a_rs,
     one_b_ss, one_b_rs, two_a_ss, two_a_rs, two_b_ss, two_b_rs, fin_ss, fin_rs, sib_ss, sib_rs,
@@ -311,10 +311,6 @@
                         part[(h, *place_at, pl.ds(offset, length), slice(None))] = jnp.zeros(
                             (length, half), BF16
                         )
-    for k in range(9):
-        kernel_t[pl.ds(k * state_width, state_width), :] = kernel[
-            pl.ds((8 - k) * channels, channels), :
-        ].T
     for copies in gd_copies:
         for copy in copies:
             copy.wait_recv()
@@ -399,15 +395,18 @@
     for f in range(frames_here):
         place(drive_taps, f, 0, drive_halo[0, f], rows, width)
         place(drive_taps, f, rows + 1, drive_halo[1, f], rows, width)
-    spread = jnp.dot(drive_taps[...], kernel_t[...], preferred_element_type=F32)
     for f in range(frames_here):
-        spread_bf[f] = (
-            spread[f * band_cells : (f + 1) * band_cells]
-            + feedthrough[...] * cotangent[f].astype(F32)
-        ).astype(BF16)
-
-    out_copies = [pltpu.make_async_copy(spread_bf, grad_frames, load_sems.at[7])]
-    out_copies[0].start()
+        spread = feedthrough[...] * cotangent[f].astype(F32)
+        for k in range(9):
+            spread = spread + lax.dot_general(
+                drive_taps[
+                    pl.ds(f * band_cells, band_cells), pl.ds(k * state_width, state_width)
+                ],
+                kernel[pl.ds((8 - k) * channels, channels), :],
+                (((1,), (1,)), ((), ())),
+                preferred_element_type=F32,
+            )
+        grad_frames[f] = spread.astype(BF16)
 
     def second_sum(one, recv1, total, own, count, send, recv, ss, rs, where):
         summed = total[...]
@@ -471,27 +470,20 @@
         sib_copies[d].start()
     for copy in sib_copies:
         copy.wait_recv()
-    out_copies.append(pltpu.make_async_copy(final, gathered, load_sems.at[8]))
-    out_copies[1].start()
     for copy in fin_copies + sib_copies:
         copy.wait_send()
-    for copy in out_copies:
-        copy.wait()
 
 
 def finish(
     dims,
-    spread, gathered, grad_frames, grad_kernel, grad_readout,
-    final, scaled, scaled_readout, sems,
+    spread, final, grad_frames, grad_kernel, grad_readout,
+    scaled, scaled_readout, sems,
 ):
     chips, slots_a, block_a, block_b, in_a, in_b, scaling = dims
     rows_here, state_width = scaled_readout.shape
     half = state_width // 2
     through = pltpu.make_async_copy(spread, grad_frames, sems.at[0])
-    load = pltpu.make_async_copy(gathered, final, sems.at[1])
-    load.start()
     through.start()
-    load.wait()
     for k in range(10):
         slot, block, begin = (in_a[k], block_a, 0) if k in in_a else (in_b[k], block_b, block_a)
         for j, offset, at, length in pieces(slot * rows_here, rows_here, block):
@@ -503,8 +495,8 @@
                 else:
                     scaled_readout[pl.ds(at, length), lanes] = value
     stores = [
-        pltpu.make_async_copy(scaled, grad_kernel, sems.at[2]),
-        pltpu.make_async_copy(scaled_readout, grad_readout, sems.at[3]),
+        pltpu.make_async_copy(scaled, grad_kernel, sems.at[1]),
+        pltpu.make_async_copy(scaled_readout, grad_readout, sems.at[2]),
     ]
     for store in stores:
         store.start()
@@ -531,6 +523,7 @@
     vmem = pltpu.VMEM
     dma = pltpu.SemaphoreType.DMA
     any_space = pl.BlockSpec(memory_space=pl.ANY)
+    whole = pl.BlockSpec(memory_space=pltpu.VMEM)
     hbm = pl.BlockSpec(memory_space=pltpu.HBM)
     every = frames_here * cells
     scratch = [
@@ -541,11 +534,10 @@
         vmem((1, channels), F32),
         vmem(decay_rate.shape, F32),
         vmem((cells, state_width), F32),
-        dma((9,)),
+        dma((7,)),
         vmem((every, 9 * channels), BF16),
         vmem((9 * channels, every), BF16),
-        vmem((9 * state_width, channels), BF16),
-        vmem((every, 9 * state_width), BF16),
+                vmem((every, 9 * state_width), BF16),
         vmem((2, frames_here, width, channels), BF16),
         vmem((2, frames_here, width, state_width), BF16),
         vmem((8, state_width), F32),
@@ -575,8 +567,6 @@
         vmem((chips, block_b, half), BF16),
         vmem((nz - 1, block_a, half), BF16),
         vmem((chips - 1, block_b, half), BF16),
-        vmem((n, block_a + block_b, half), BF16),
-        vmem((frames_here, cells, channels), BF16),
     ]
     counts = ((2,), (n - 1,), (groups, n - 1), (groups, n - 1), (groups, n - 1), (2,))
     counts += ((chips,), (nz,), (chips - 1,), (nz - 1,), (nz - 1,), (chips - 1,))
@@ -585,14 +575,14 @@
     spread, gathered = pl.pallas_call(
         functools.partial(fused, (n, nz, slots_a, slots_b, groups)),
         out_shape=(
-            jax.ShapeDtypeStruct((frames_here, cells, channels), BF16),
-            jax.ShapeDtypeStruct((n, block_a + block_b, half), BF16),
+            vmem((frames_here, cells, channels), BF16),
+            vmem((n, block_a + block_b, half), BF16),
         ),
         in_specs=[hbm] * 7,
-        out_specs=(hbm, hbm),
+        out_specs=(whole, whole),
         scratch_shapes=scratch,
         compiler_params=pltpu.CompilerParams(
-            collective_id=0, has_side_effects=True, vmem_limit_bytes=60 * 1024 * 1024
+            collective_id=0, has_side_effects=True, vmem_limit_bytes=48 * 1024 * 1024
         ),
         cost_estimate=pl.CostEstimate(
             flops=2 * every * channels * state_width * 30,
@@ -601,13 +591,18 @@
         ),
         name="conv_s5_backward",
     )(
-        frames_in,
-        cotangent.reshape(frames_here, cells, channels),
-        kernel.reshape(9 * channels, state_width),
-        readout,
-        feedthrough.reshape(1, channels),
-        decay_rate,
-        start_state.reshape(cells, state_width),
+        *(
+            pltpu.with_memory_space_constraint(argument, pltpu.HBM)
+            for argument in (
+                frames_in,
+                cotangent.reshape(frames_here, cells, channels),
+                kernel.reshape(9 * channels, state_width),
+                readout,
+                feedthrough.reshape(1, channels),
+                decay_rate,
+                start_state.reshape(cells, state_width),
+            )
+        )
     )
     in_a, in_b = places(slots_a)
     spread, kernel_part, readout_part = pl.pallas_call(
@@ -617,15 +612,14 @@
             jax.ShapeDtypeStruct((9, rows_here, state_width), F32),
             jax.ShapeDtypeStruct((rows_here, state_width), F32),
         ),
-        in_specs=[any_space] * 2,
+        in_specs=[whole] * 2,
         out_specs=(any_space,) * 3,
         scratch_shapes=[
-            vmem((n, block_a + block_b, half), BF16),
             vmem((9, rows_here, state_width), F32),
             vmem((rows_here, state_width), F32),
-            dma((4,)),
+            dma((3,)),
         ],
-        compiler_params=pltpu.CompilerParams(vmem_limit_bytes=60 * 1024 * 1024),
+        compiler_params=pltpu.CompilerParams(vmem_limit_bytes=48 * 1024 * 1024),
         name="write_outputs",
     )(spread, gathered)
     return (spread.reshape(frames_in.shape), kernel_part, readout_part.T)

time: 50.3 us -> 41.5 us (0.83); the launches traced: 49.5 us -> 41.3 us
  Pallas kernels: 48.9 us -> 40.6 us
    pallas_call x1, Pallas kernels: 9.08 us -> 0.94 us  [local(): pl.pallas_call(functools.partial(finish, (chips, slots_a, block_a, block_...]
where the time goes in v4:
time: 41.5 us; the launch traced here: 41.3 us
  Pallas kernels  40.6 us (98%)
  between operations  0.64 us (2%)
    pallas_call x1, Pallas kernels, local(): pl.pallas_call(functools.partial(fused, (n, nz, slots_a, slots_b, groups)...  39.7 us
    pallas_call x1, Pallas kernels, local(): pl.pallas_call(functools.partial(finish, (chips, slots_a, block_a, block_...  0.94 us

profile of v4, /device:TPU:0, one launch (start us, length us, event | category | flops | bytes accessed | tf_op | source)
XLA Modules:
  0.0 41.3 jit_solution(13054153031955102860)
XLA Ops:
  0.6 39.7 %conv_s5_backward.1 = (bf16[2,256,256]{2,1,0:T(8,128)(2,1)S(1)}, bf16[8,160,128]{2,1,0:T(8,128)(2,1)S(1)}) custom-call(bf16[2,4,64,256]{3,2,1,0:T(8,128)(2,1)} %frames_hbm.1, bf16[2,256,256]{2,1,0:T(8,128)(2,1)} %bitcast.7, bf16[2304,256]{1,0:T(8,128)(2,1)} %bitcast.6, bf16[256,256]{1,0:T(8,128)(2,1)} %readout_hbm.1, f32[1,256]{1,0:T(1,128)} %bitcast.11, ...), custom_call_target="tpu_custom_call" | custom-call | flops 2013265920 | bytes 6291456 | tf_op jit(solution)/shard_map/conv_s5_backward/pallas_call | solution.py:575
  40.3 0.9 %write_outputs.1 = (bf16[2,256,256]{2,1,0:T(8,128)(2,1)}, f32[9,64,256]{2,1,0:T(8,128)}, f32[64,256]{1,0:T(8,128)}) custom-call(bf16[2,256,256]{2,1,0:T(8,128)(2,1)S(1)} %get-tuple-element.8.spread, bf16[8,160,128]{2,1,0:T(8,128)(2,1)S(1)} %get-tuple-element.9.final), custom_call_target="tpu_custom_call" | custom-call | tf_op jit(solution)/shard_map/write_outputs/pallas_call | solution.py:608

commit v5 on v4

--- a/solution.py
+++ b/solution.py
@@ -23,7 +23,7 @@
     )
 
 
-def place(taps, frame, padded_row, cells, rows, width):
+def place(taps, row_at, frame, padded_row, cells, rows, width):
     channels = cells.shape[1]
     wide = cells.astype(F32)
     column = lax.broadcasted_iota(jnp.int32, wide.shape, 0)
@@ -35,7 +35,7 @@
             if 0 <= h < rows:
                 k = 3 * i + j
                 taps[
-                    pl.ds((frame * rows + h) * width, width), pl.ds(k * channels, channels)
+                    pl.ds(row_at(frame, h), width), pl.ds(k * channels, channels)
                 ] = shifted
 
 
@@ -63,7 +63,7 @@
     taps, taps_t, drive_taps,
     halo, drive_halo, own_decay, all_decay,
     cot_send, cot_recv, driven, drv_send, drv_recv,
-    states_bf, slopes, pulled, gd_send, gd_recv, drive,
+    states_bf, slopes, pulled, gd_send, gd_recv, drive, drive_flat,
     grads_a, grads_b, pair_a, pair_b, send1_a, send1_b, recv1_a, recv1_b, total_a, total_b,
     send2_a, send2_b, recv2_a, recv2_b,
     halo_ss, halo_rs, dec_ss, dec_rs, cot_ss, cot_rs, drv_ss, drv_rs, gd_ss, gd_rs,
@@ -160,7 +160,6 @@
 
     edge_start(frames_hbm, halo, halo_ss, halo_rs)
     loads[1].wait()
-    loads[2].wait()
     def over_tm(src_of, dst, ss, rs):
         copies = []
         for d in range(1, n):
@@ -170,44 +169,53 @@
             )
         return copies
 
+    group_cells = band_cells // groups
+    group_rows = rows // groups
+
     def cells_of(s, g):
-        begin = s * share + g * part_cells
+        begin = g * group_cells + s * part_cells
         return slice(begin, begin + part_cells)
 
-    for g in range(groups):
-        for s in range(n):
-            cot_send[g, s] = jnp.concatenate(
-                [cotangent[f, cells_of(s, g), :] for f in range(frames_here)], axis=0
-            )
-        cot_recv[g, me] = cot_send[g, me]
+    def row_at(f, h):
+        return ((h // group_rows * frames_here + f) * group_rows + h % group_rows) * width
+
+    def in_group(g):
+        return pl.ds(g * frames_here * group_cells, frames_here * group_cells)
+
 
     dec_copies = over_tm(lambda to: own_decay, all_decay, dec_ss, dec_rs)
     for copy in dec_copies:
         copy.start()
-    cot_copies = []
-    for g in range(groups):
-        cot_copies.append(
-            over_tm(
-                lambda to, g=g: cot_send.at[g, to], cot_recv.at[g], cot_ss.at[g], cot_rs.at[g]
-            )
-        )
-        for copy in cot_copies[g]:
-            copy.start()
-
     for f in range(frames_here):
         for r in range(rows):
-            place(taps, f, r + 1, frames[f, r], rows, width)
+            place(taps, row_at, f, r + 1, frames[f, r], rows, width)
+    loads[2].wait()
+    for s in range(n):
+        for g in range(groups):
+            cot_send[s, g] = jnp.concatenate(
+                [cotangent[f, cells_of(s, g), :] for f in range(frames_here)], axis=0
+            )
+    cot_copies = over_tm(lambda to: cot_send.at[to], cot_recv, cot_ss, cot_rs)
+    for copy in cot_copies:
+        copy.start()
+    cot_recv[me] = cot_send[me]
     edge_wait(frames_hbm, halo, halo_ss, halo_rs, True)
     for f in range(frames_here):
-        place(taps, f, 0, halo[0, f], rows, width)
-        place(taps, f, rows + 1, halo[1, f], rows, width)
+        place(taps, row_at, f, 0, halo[0, f], rows, width)
+        place(taps, row_at, f, rows + 1, halo[1, f], rows, width)
     loads[3].wait()
-    driven[...] = jnp.dot(taps[...], kernel[...], preferred_element_type=F32).reshape(driven.shape)
     drv_copies = []
     for g in range(groups):
+        driven[g] = jnp.dot(
+            taps[in_group(g), :], kernel[...], preferred_element_type=F32
+        ).reshape(driven.shape[1:])
         for s in range(n):
             drv_send[g, s] = jnp.concatenate(
-                [driven[f, cells_of(s, g), :] for f in range(frames_here)], axis=0
+                [
+                    driven[g, f, s * part_cells : (s + 1) * part_cells, :]
+                    for f in range(frames_here)
+                ],
+                axis=0,
             ).astype(BF16)
         drv_copies.append(
             over_tm(
@@ -218,9 +226,11 @@
             copy.start()
         drv_recv[g, me] = drv_send[g, me]
 
-    for k in range(9):
-        taps_t[pl.ds(k * channels, channels), :] = taps[:, pl.ds(k * channels, channels)].T
-
+    def transpose_taps(first, last):
+        for k in range(first, last):
+            taps_t[pl.ds(k * channels, channels), :] = taps[:, pl.ds(k * channels, channels)].T
+
+    transpose_taps(0, 4)
     for load in loads[4:7]:
         load.wait()
 
@@ -231,7 +241,7 @@
     for g in range(groups):
         for copy in drv_copies[g]:
             copy.wait_recv()
-        begin = pl.multiple_of(me * share + g * part_cells, part_cells)
+        begin = pl.multiple_of(g * group_cells + me * part_cells, part_cells)
         state = start_state[pl.ds(begin, part_cells), :]
         for s in range(n):
             arrived = drv_recv[g, s].astype(F32)
@@ -242,13 +252,14 @@
                 state = rate * state + gain * arrived[f * part_cells : (f + 1) * part_cells]
                 kept.append(state)
             states_bf[g, s] = jnp.concatenate(kept, axis=0).astype(BF16)
-        for copy in cot_copies[g]:
-            copy.wait_recv()
+        if g == 0:
+            for copy in cot_copies:
+                copy.wait_recv()
         mixture = jnp.dot(
             states_bf[g].reshape(flat, state_width), readout[...], preferred_element_type=F32
         )
         slopes[g] = (
-            cot_recv[g].reshape(flat, channels).astype(F32) * gelu_slope(mixture)
+            cot_recv[:, g].reshape(flat, channels).astype(F32) * gelu_slope(mixture)
         ).astype(BF16)
         pulled[...] = lax.dot_general(
             slopes[g], readout[...], (((1,), (1,)), ((), ())), preferred_element_type=F32
@@ -311,24 +322,26 @@
                         part[(h, *place_at, pl.ds(offset, length), slice(None))] = jnp.zeros(
                             (length, half), BF16
                         )
+    transpose_taps(4, 9)
     for copies in gd_copies:
         for copy in copies:
             copy.wait_recv()
-    for f in range(frames_here):
-        drive[f] = (
-            jnp.concatenate(
+    for g in range(groups):
+        for f in range(frames_here):
+            back = jnp.concatenate(
                 [
                     gd_recv[g, s, f * part_cells : (f + 1) * part_cells, :].astype(F32)
                     for s in range(n)
-                    for g in range(groups)
                 ],
                 axis=0,
-            )
-            .astype(BF16)
-            .reshape(rows, width, state_width)
-        )
+            ).astype(BF16)
+            drive_flat[pl.ds((g * frames_here + f) * group_cells, group_cells), :] = back
+            drive[f, g * group_rows : (g + 1) * group_rows] = back.reshape(
+                group_rows, width, state_width
+            )
     edge_start(drive, drive_halo, dhalo_ss, dhalo_rs)
-    flat_drive = drive[...].reshape(frames_here * band_cells, state_width)
+    flat_drive = drive_flat[...]
+
     def tap_gradient(k):
         keep(
             k,
@@ -390,23 +403,31 @@
 
     for f in range(frames_here):
         for r in range(rows):
-            place(drive_taps, f, r + 1, drive[f, r], rows, width)
+            place(drive_taps, row_at, f, r + 1, drive[f, r], rows, width)
     edge_wait(drive, drive_halo, dhalo_ss, dhalo_rs, True)
     for f in range(frames_here):
-        place(drive_taps, f, 0, drive_halo[0, f], rows, width)
-        place(drive_taps, f, rows + 1, drive_halo[1, f], rows, width)
-    for f in range(frames_here):
-        spread = feedthrough[...] * cotangent[f].astype(F32)
+        place(drive_taps, row_at, f, 0, drive_halo[0, f], rows, width)
+        place(drive_taps, row_at, f, rows + 1, drive_halo[1, f], rows, width)
+    for g in range(groups):
+        spread = jnp.concatenate(
+            [
+                feedthrough[...]
+                * cotangent[f, g * group_cells : (g + 1) * group_cells, :].astype(F32)
+                for f in range(frames_here)
+            ],
+            axis=0,
+        )
         for k in range(9):
             spread = spread + lax.dot_general(
-                drive_taps[
-                    pl.ds(f * band_cells, band_cells), pl.ds(k * state_width, state_width)
-                ],
+                drive_taps[in_group(g), pl.ds(k * state_width, state_width)],
                 kernel[pl.ds((8 - k) * channels, channels), :],
                 (((1,), (1,)), ((), ())),
                 preferred_element_type=F32,
             )
-        grad_frames[f] = spread.astype(BF16)
+        for f in range(frames_here):
+            grad_frames[f, g * group_cells : (g + 1) * group_cells, :] = spread[
+                f * group_cells : (f + 1) * group_cells
+            ].astype(BF16)
 
     def second_sum(one, recv1, total, own, count, send, recv, ss, rs, where):
         summed = total[...]
@@ -457,7 +478,7 @@
         copy.start()
     sib_copies[0].start()
     flat_copies = dec_copies
-    for copies in cot_copies + drv_copies + gd_copies:
+    for copies in [cot_copies] + drv_copies + gd_copies:
         flat_copies = flat_copies + copies
     for copies in (pair_a_copies, pair_b_copies, one_a, one_b, two_a, two_b):
         flat_copies = flat_copies + copies
@@ -517,7 +538,7 @@
     slots_b = -(-max(10 - slots_a, 1) // step) * step
     block_a = slots_a * rows_here // chips
     block_b = slots_b * rows_here // chips
-    groups = 2 if frames_here * share // 2 % 16 == 0 and share % 16 == 0 else 1
+    groups = 2 if frames_here * share // 2 % 16 == 0 and share % 16 == 0 and rows % 2 == 0 else 1
     mixed = frames_here * share // groups
     scaling = 1.0 / math.sqrt(frames_here * cells * n * nz)
     vmem = pltpu.VMEM
@@ -542,9 +563,9 @@
         vmem((2, frames_here, width, state_width), BF16),
         vmem((8, state_width), F32),
         vmem((n, 8, state_width), F32),
-        vmem((groups, n, mixed, channels), BF16),
-        vmem((groups, n, mixed, channels), BF16),
-        vmem((frames_here, cells, state_width), F32),
+        vmem((n, groups, mixed, channels), BF16),
+        vmem((n, groups, mixed, channels), BF16),
+        vmem((groups, frames_here, cells // groups, state_width), F32),
         vmem((groups, n, mixed, state_width), BF16),
         vmem((groups, n, mixed, state_width), BF16),
         vmem((groups, n, mixed, state_width), BF16),
@@ -553,6 +574,7 @@
         vmem((groups, n, mixed, state_width), BF16),
         vmem((groups, n, mixed, state_width), BF16),
         vmem((frames_here, rows, width, state_width), BF16),
+        vmem((every, state_width), BF16),
         vmem((2, chips, nz, block_a, half), BF16),
         vmem((2, nz, chips, block_b, half), BF16),
         vmem((chips, nz, block_a, half), BF16),
@@ -568,7 +590,7 @@
         vmem((nz - 1, block_a, half), BF16),
         vmem((chips - 1, block_b, half), BF16),
     ]
-    counts = ((2,), (n - 1,), (groups, n - 1), (groups, n - 1), (groups, n - 1), (2,))
+    counts = ((2,), (n - 1,), (n - 1,), (groups, n - 1), (groups, n - 1), (2,))
     counts += ((chips,), (nz,), (chips - 1,), (nz - 1,), (nz - 1,), (chips - 1,))
     for count in counts + ((chips - 1,), (chips,)):
         scratch += [dma(count), dma(count)]

time: 41.5 us -> 40.7 us (0.981)
  Pallas kernels: 40.6 us -> 39.9 us
    pallas_call x1, Pallas kernels: 39.7 us -> 39 us  [local(): pl.pallas_call(functools.partial(fused, (n, nz, slots_a, slots_b, groups)...]
where the time goes in v5:
time: 40.7 us; the launch traced here: 40.6 us
  Pallas kernels  39.9 us (98%)
  between operations  0.64 us (2%)
    pallas_call x1, Pallas kernels, local(): pl.pallas_call(functools.partial(fused, (n, nz, slots_a, slots_b, groups)...  39 us
    pallas_call x1, Pallas kernels, local(): pl.pallas_call(functools.partial(finish, (chips, slots_a, block_a, block_...  0.94 us

profile of v5, /device:TPU:0, one launch (start us, length us, event | category | flops | bytes accessed | tf_op | source)
XLA Modules:
  0.0 40.6 jit_solution(560211236856983585)
XLA Ops:
  0.6 39.0 %conv_s5_backward.1 = (bf16[2,256,256]{2,1,0:T(8,128)(2,1)S(1)}, bf16[8,160,128]{2,1,0:T(8,128)(2,1)S(1)}) custom-call(bf16[2,4,64,256]{3,2,1,0:T(8,128)(2,1)} %frames_hbm.1, bf16[2,256,256]{2,1,0:T(8,128)(2,1)} %bitcast.7, bf16[2304,256]{1,0:T(8,128)(2,1)} %bitcast.6, bf16[256,256]{1,0:T(8,128)(2,1)} %readout_hbm.1, f32[1,256]{1,0:T(1,128)} %bitcast.11, ...), custom_call_target="tpu_custom_call" | custom-call | flops 2013265920 | bytes 6291456 | tf_op jit(solution)/shard_map/conv_s5_backward/pallas_call | solution.py:597
  39.6 0.9 %write_outputs.1 = (bf16[2,256,256]{2,1,0:T(8,128)(2,1)}, f32[9,64,256]{2,1,0:T(8,128)}, f32[64,256]{1,0:T(8,128)}) custom-call(bf16[2,256,256]{2,1,0:T(8,128)(2,1)S(1)} %get-tuple-element.8.spread, bf16[8,160,128]{2,1,0:T(8,128)(2,1)S(1)} %get-tuple-element.9.final), custom_call_target="tpu_custom_call" | custom-call | tf_op jit(solution)/shard_map/write_outputs/pallas_call | solution.py:630

commit v6 on v5

--- a/solution.py
+++ b/solution.py
@@ -199,16 +199,30 @@
     for copy in cot_copies:
         copy.start()
     cot_recv[me] = cot_send[me]
+    rim_taps = ((0, 0, pl.ds(0, 3 * channels)), (1, rows - 1, pl.ds(6 * channels, 3 * channels)))
+    for _, h, columns in rim_taps:
+        for f in range(frames_here):
+            taps[pl.ds(row_at(f, h), width), columns] = jnp.zeros((width, 3 * channels), BF16)
+    loads[3].wait()
+    for g in range(groups):
+        driven[g] = jnp.dot(
+            taps[in_group(g), :], kernel[...], preferred_element_type=F32
+        ).reshape(driven.shape[1:])
     edge_wait(frames_hbm, halo, halo_ss, halo_rs, True)
     for f in range(frames_here):
         place(taps, row_at, f, 0, halo[0, f], rows, width)
         place(taps, row_at, f, rows + 1, halo[1, f], rows, width)
-    loads[3].wait()
     drv_copies = []
     for g in range(groups):
-        driven[g] = jnp.dot(
-            taps[in_group(g), :], kernel[...], preferred_element_type=F32
-        ).reshape(driven.shape[1:])
+        for _, h, columns in rim_taps:
+            if h // group_rows == g:
+                rim = jnp.concatenate(
+                    [taps[pl.ds(row_at(f, h), width), columns] for f in range(frames_here)], axis=0
+                )
+                added = jnp.dot(rim, kernel[columns, :], preferred_element_type=F32)
+                at = pl.ds(h % group_rows * width, width)
+                for f in range(frames_here):
+                    driven[g, f, at, :] += added[f * width : (f + 1) * width]
         for s in range(n):
             drv_send[g, s] = jnp.concatenate(
                 [
@@ -367,22 +381,34 @@
         if k in in_b:
             tap_gradient(k)
     pair_b_copies = over_pair(grads_b, pair_b, band, nz, pairb_ss, pairb_rs)
+    pair_a_copies = [
+        remote(
+            grads_a.at[1 - core, j], pair_a.at[j], paira_ss.at[j], paira_rs.at[j],
+            {"tm": me + 1 - 2 * core},
+        )
+        for j in range(chips)
+    ]
+    sent = 0
     for k in range(9):
         if k in in_a:
             tap_gradient(k)
-    pair_a_copies = over_pair(grads_a, pair_a, chip, chips, paira_ss, paira_rs)
-
-    def first_sum(pair_copies, grads, pair, own, count, send, recv, ss, rs, where, total):
+            while (sent + 1) * block_a <= (in_a[k] + 1) * rows_here:
+                pair_a_copies[sent].start()
+                sent += 1
+    for copy in pair_a_copies[sent:]:
+        copy.start()
+
+    def first_sum(arrive, grads, pair, own, count, send, recv, ss, rs, where, total):
         copies = []
         for d in range(1, count):
             at = lax.rem(own + d, count)
-            pair_copies[d - 1].wait_recv()
+            arrive(d, at)
             send[d - 1] = (grads[core, at].astype(F32) + pair[at].astype(F32)).astype(BF16)
             copies.append(
                 remote(send.at[d - 1], recv.at[d - 1], ss.at[d - 1], rs.at[d - 1], where(at))
             )
             copies[-1].start()
-        pair_copies[-1].wait_recv()
+        arrive(0, own)
         total[...] = grads[core, own].astype(F32) + pair[own].astype(F32)
         return copies
 
@@ -392,12 +418,18 @@
     def to_band(z):
         return {"row": z}
 
+    def arrive_a(d, at):
+        remote(
+            grads_a.at[1 - core, at], pair_a.at[at], paira_ss.at[at], paira_rs.at[at],
+            {"tm": me + 1 - 2 * core},
+        ).wait_recv()
+
     one_b = first_sum(
-        pair_b_copies, grads_b, pair_b, band, nz, send1_b, recv1_b, one_b_ss, one_b_rs,
+        lambda d, at: pair_b_copies[d - 1].wait_recv(), grads_b, pair_b, band, nz, send1_b, recv1_b, one_b_ss, one_b_rs,
         to_band, total_b,
     )
     one_a = first_sum(
-        pair_a_copies, grads_a, pair_a, chip, chips, send1_a, recv1_a, one_a_ss, one_a_rs,
+        arrive_a, grads_a, pair_a, chip, chips, send1_a, recv1_a, one_a_ss, one_a_rs,
         to_chip, total_a,
     )
 

time: 40.7 us -> 40.2 us (0.988)
  Pallas kernels: 39.9 us -> 39.4 us
    pallas_call x1, Pallas kernels: 39 us -> 38.4 us  [local(): pl.pallas_call(functools.partial(fused, (n, nz, slots_a, slots_b, groups)...]
where the time goes in v6:
time: 40.2 us; the launch traced here: 40 us
  Pallas kernels  39.4 us (98%)
  between operations  0.64 us (2%)
    pallas_call x1, Pallas kernels, local(): pl.pallas_call(functools.partial(fused, (n, nz, slots_a, slots_b, groups)...  38.4 us
    pallas_call x1, Pallas kernels, local(): pl.pallas_call(functools.partial(finish, (chips, slots_a, block_a, block_...  0.94 us

profile of v6, /device:TPU:0, one launch (start us, length us, event | category | flops | bytes accessed | tf_op | source)
XLA Modules:
  0.0 40.0 jit_solution(15694929921237858229)
XLA Ops:
  0.6 38.4 %conv_s5_backward.1 = (bf16[2,256,256]{2,1,0:T(8,128)(2,1)S(1)}, bf16[8,160,128]{2,1,0:T(8,128)(2,1)S(1)}) custom-call(bf16[2,4,64,256]{3,2,1,0:T(8,128)(2,1)} %frames_hbm.1, bf16[2,256,256]{2,1,0:T(8,128)(2,1)} %bitcast.7, bf16[2304,256]{1,0:T(8,128)(2,1)} %bitcast.6, bf16[256,256]{1,0:T(8,128)(2,1)} %readout_hbm.1, f32[1,256]{1,0:T(1,128)} %bitcast.11, ...), custom_call_target="tpu_custom_call" | custom-call | flops 2013265920 | bytes 6291456 | tf_op jit(solution)/shard_map/conv_s5_backward/pallas_call | solution.py:629
  39.1 0.9 %write_outputs.1 = (bf16[2,256,256]{2,1,0:T(8,128)(2,1)}, f32[9,64,256]{2,1,0:T(8,128)}, f32[64,256]{1,0:T(8,128)}) custom-call(bf16[2,256,256]{2,1,0:T(8,128)(2,1)S(1)} %get-tuple-element.8.spread, bf16[8,160,128]{2,1,0:T(8,128)(2,1)S(1)} %get-tuple-element.9.final), custom_call_target="tpu_custom_call" | custom-call | tf_op jit(solution)/shard_map/write_outputs/pallas_call | solution.py:662

commit v7 on v6

--- a/solution.py
+++ b/solution.py
@@ -388,16 +388,6 @@
         )
         for j in range(chips)
     ]
-    sent = 0
-    for k in range(9):
-        if k in in_a:
-            tap_gradient(k)
-            while (sent + 1) * block_a <= (in_a[k] + 1) * rows_here:
-                pair_a_copies[sent].start()
-                sent += 1
-    for copy in pair_a_copies[sent:]:
-        copy.start()
-
     def first_sum(arrive, grads, pair, own, count, send, recv, ss, rs, where, total):
         copies = []
         for d in range(1, count):
@@ -424,10 +414,22 @@
             {"tm": me + 1 - 2 * core},
         ).wait_recv()
 
-    one_b = first_sum(
-        lambda d, at: pair_b_copies[d - 1].wait_recv(), grads_b, pair_b, band, nz, send1_b, recv1_b, one_b_ss, one_b_rs,
-        to_band, total_b,
-    )
+    early = min(3, len(in_a)) - 1
+    sent = 0
+    for k in range(9):
+        if k in in_a:
+            tap_gradient(k)
+            while (sent + 1) * block_a <= (in_a[k] + 1) * rows_here:
+                pair_a_copies[sent].start()
+                sent += 1
+            if in_a[k] == early:
+                one_b = first_sum(
+                    lambda d, at: pair_b_copies[d - 1].wait_recv(),
+                    grads_b, pair_b, band, nz, send1_b, recv1_b, one_b_ss, one_b_rs,
+                    to_band, total_b,
+                )
+    for copy in pair_a_copies[sent:]:
+        copy.start()
     one_a = first_sum(
         arrive_a, grads_a, pair_a, chip, chips, send1_a, recv1_a, one_a_ss, one_a_rs,
         to_chip, total_a,
@@ -566,7 +568,7 @@
     rows_here = channels // nz
     half = state_width // 2
     step = 16 * chips // math.gcd(rows_here, 16 * chips)
-    slots_a = -(-7 // step) * step
+    slots_a = -(-6 // step) * step
     slots_b = -(-max(10 - slots_a, 1) // step) * step
     block_a = slots_a * rows_here // chips
     block_b = slots_b * rows_here // chips

time: 40.2 us -> 39.9 us (level)
  no operation moved by 1% of the time
where the time goes in v7:
time: 39.9 us; the launch traced here: 39.8 us
  Pallas kernels  39.1 us (98%)
  between operations  0.64 us (2%)
    pallas_call x1, Pallas kernels, local(): pl.pallas_call(functools.partial(fused, (n, nz, slots_a, slots_b, groups)...  38.2 us
    pallas_call x1, Pallas kernels, local(): pl.pallas_call(functools.partial(finish, (chips, slots_a, block_a, block_...  0.94 us

profile of v7, /device:TPU:0, one launch (start us, length us, event | category | flops | bytes accessed | tf_op | source)
XLA Modules:
  0.0 39.8 jit_solution(11861835131054126434)
XLA Ops:
  0.6 38.2 %conv_s5_backward.1 = (bf16[2,256,256]{2,1,0:T(8,128)(2,1)S(1)}, bf16[8,160,128]{2,1,0:T(8,128)(2,1)S(1)}) custom-call(bf16[2,4,64,256]{3,2,1,0:T(8,128)(2,1)} %frames_hbm.1, bf16[2,256,256]{2,1,0:T(8,128)(2,1)} %bitcast.7, bf16[2304,256]{1,0:T(8,128)(2,1)} %bitcast.6, bf16[256,256]{1,0:T(8,128)(2,1)} %readout_hbm.1, f32[1,256]{1,0:T(1,128)} %bitcast.11, ...), custom_call_target="tpu_custom_call" | custom-call | flops 2013265920 | bytes 6291456 | tf_op jit(solution)/shard_map/conv_s5_backward/pallas_call | solution.py:631
  38.8 0.9 %write_outputs.1 = (bf16[2,256,256]{2,1,0:T(8,128)(2,1)}, f32[9,64,256]{2,1,0:T(8,128)}, f32[64,256]{1,0:T(8,128)}) custom-call(bf16[2,256,256]{2,1,0:T(8,128)(2,1)S(1)} %get-tuple-element.8.spread, bf16[8,160,128]{2,1,0:T(8,128)(2,1)S(1)} %get-tuple-element.9.final), custom_call_target="tpu_custom_call" | custom-call | tf_op jit(solution)/shard_map/write_outputs/pallas_call | solution.py:664
